TPU v7x, 512 devices: a whole 4x8x8 slice. The times are simulated.
512 devices in a mesh: gx: 8 (over y_hi, x), gy: 4 (over y_lo), gz: 16 (over z, core).
Axes of the slice: x: 4, y: 8 (y_hi: 2, y_lo: 4; y = y_hi * 4 + y_lo), z: 8, core: 2. Of those that a mesh axis runs over, the one named last changes fastest.
Arguments:
- design: float32 [64, 32, 4096], P('gx', 'gy', 'gz'), may hold values from 0 to 1
- flags: int32 [64, 32, 4096], P('gx', 'gy', 'gz'), may hold values from 0 to 7
- displacement: float32 [3, 64, 32, 4096], P(None, 'gx', 'gy', 'gz'), may hold values from -6 to 6
- adjoint: float32 [3, 64, 32, 4096], P(None, 'gx', 'gy', 'gz'), may hold values from -6 to 6
- pressure: float32 [64, 32, 4096], P('gx', 'gy', 'gz'), may hold values from -6 to 6
- multiplier: float32 [64, 32, 4096], P('gx', 'gy', 'gz'), may hold values from -6 to 6
Outputs:
- sensitivity: float32 [64, 32, 4096], P('gx', 'gy', 'gz')
Inputs may be any that keep to these rules, and one draw needn't show every extreme that they name: `flags`: 0 marks a passive void element, 1 a passive solid one, every other value a design element.
All inputs are finite; a program needn't handle non-finite values.
Results may differ from a plain program's by a relative error of at most 0.00019.
Values sent between devices are 32-bit elements; how exact they have to be, the bound alone decides.
A program may use at most 64 MiB of HBM per device.

v0:
```python
import math

import jax
import jax.numpy as jnp
import numpy as np
from jax import lax
from jax.sharding import PartitionSpec as P

poisson = 0.45
sharpness = 4.0
threshold = 0.5
stiff_floor = 0.001
cone_radius = 3.5


def from_behind(value, axis, by):
    peers = lax.axis_size(axis)
    pairs = [(i, i + by) for i in range(peers) if 0 <= i + by < peers]
    return lax.ppermute(value, axis, pairs)


def with_halo(cells, sides, width):
    for axis, dim in sides:
        count = lax.axis_size(axis)
        ends = count - 1
        head = lax.slice_in_dim(cells, 0, width, axis=dim)
        tail = lax.slice_in_dim(cells, cells.shape[dim] - width, cells.shape[dim], axis=dim)
        cells = jnp.concatenate(
            [
                lax.ppermute(tail, axis, [(i, (i + 1) % count) for i in range(ends)]),
                cells,
                lax.ppermute(head, axis, [((i + 1) % count, i) for i in range(ends)]),
            ],
            axis=dim,
        )
    return cells


def element_tables():
    root = 1.0 / np.sqrt(3.0)
    points = [(1.0 - root) / 2.0, (1.0 + root) / 2.0]
    shear = 1.0 / (2.0 * (1.0 + poisson))
    project = np.zeros((6, 6))
    for place, entry in enumerate([1.0, 1.0, 1.0, 0.5, 0.5, 0.5]):
        project[place, place] = entry
    project[:3, :3] -= 1.0 / 3.0
    elastic = 2.0 * shear * project
    stiffness = np.zeros((24, 24))
    coupling = np.zeros(24)
    for point_x in points:
        for point_y in points:
            for point_z in points:
                deriv = np.zeros((3, 8))
                for corner in range(8):
                    bit_x, bit_y, bit_z = (corner & 1, corner >> 1 & 1, corner >> 2 & 1)
                    fac_x = point_x if bit_x else 1.0 - point_x
                    fac_y = point_y if bit_y else 1.0 - point_y
                    fac_z = point_z if bit_z else 1.0 - point_z
                    sig_x = 1.0 if bit_x else -1.0
                    sig_y = 1.0 if bit_y else -1.0
                    sig_z = 1.0 if bit_z else -1.0
                    deriv[0, corner] = sig_x * fac_y * fac_z
                    deriv[1, corner] = fac_x * sig_y * fac_z
                    deriv[2, corner] = fac_x * fac_y * sig_z
                strain = np.zeros((6, 24))
                for corner in range(8):
                    column = 3 * corner
                    strain[0, column] = deriv[0, corner]
                    strain[1, column + 1] = deriv[1, corner]
                    strain[2, column + 2] = deriv[2, corner]
                    strain[3, column] = deriv[1, corner]
                    strain[3, column + 1] = deriv[0, corner]
                    strain[4, column + 1] = deriv[2, corner]
                    strain[4, column + 2] = deriv[1, corner]
                    strain[5, column] = deriv[2, corner]
                    strain[5, column + 2] = deriv[0, corner]
                stiffness += 0.125 * strain.T @ elastic @ strain
                coupling += 0.125 * (strain[0] + strain[1] + strain[2])
    bulk = 1.0 / (3.0 * (1.0 - 2.0 * poisson))
    return (stiffness.astype(np.float32), coupling.astype(np.float32), float(bulk))


def cone_offsets():
    found = []
    for off_x in range(-3, 4):
        for off_y in range(-3, 4):
            for off_z in range(-3, 4):
                radius = math.sqrt(off_x * off_x + off_y * off_y + off_z * off_z)
                if radius < cone_radius:
                    found.append((off_x, off_y, off_z, cone_radius - radius))
    return found


def cone_sum(padded, count_x, count_y, count_z):
    total = jnp.zeros((count_x, count_y, count_z), jnp.float32)
    for off_x, off_y, off_z, weight in cone_offsets():
        piece = lax.slice(
            padded,
            (3 + off_x, 3 + off_y, 3 + off_z),
            (3 + off_x + count_x, 3 + off_y + count_y, 3 + off_z + count_z),
        )
        total = total + jnp.float32(weight) * piece
    return total


def element_energy(forward_ext, adjoint_ext, pressure, multiplier, count_x, count_y, count_z):
    stiff_np, coup_np, bulk = element_tables()
    stiffness = jnp.asarray(stiff_np, jnp.float32)
    coupling = jnp.asarray(coup_np, jnp.float32)

    def gather_dofs(field):
        pieces = []
        for corner in range(8):
            bit_x, bit_y, bit_z = (corner & 1, corner >> 1 & 1, corner >> 2 & 1)
            pieces.append(
                field[:, bit_x : bit_x + count_x, bit_y : bit_y + count_y, bit_z : bit_z + count_z]
            )
        return jnp.concatenate(pieces, 0)

    forward = gather_dofs(forward_ext)
    backward = gather_dofs(adjoint_ext)
    pushed = jnp.einsum("ij,jxyz->ixyz", stiffness, forward, precision=lax.Precision.HIGHEST)
    energy = jnp.sum(backward * pushed, axis=0)
    energy = (
        energy
        + jnp.einsum("j,jxyz->xyz", coupling, backward, precision=lax.Precision.HIGHEST) * pressure
    )
    energy = energy + multiplier * jnp.einsum(
        "j,jxyz->xyz", coupling, forward, precision=lax.Precision.HIGHEST
    )
    energy = energy - multiplier * pressure / jnp.float32(bulk)
    return energy


def projection(filtered, flags, energy, weight_total):
    denom = math.tanh(sharpness * threshold) + math.tanh(sharpness * (1.0 - threshold))
    hyper = jnp.tanh(sharpness * (filtered - threshold))
    smooth = (math.tanh(sharpness * threshold) + hyper) / denom
    deriv = sharpness * (1.0 - hyper * hyper) / denom
    active = flags >= 2
    projected = jnp.where(active, smooth, jnp.where(flags == 1, 1.0, 0.0))
    slope = jnp.where(active, deriv, 0.0)
    return -3.0 * projected * projected * (1.0 - stiff_floor) * energy * slope / weight_total


def axis_inside(place, parts, count):
    position = place * count - 3 + jnp.arange(count + 6, dtype=jnp.int32)
    total = count * parts
    return ((position >= 0) & (position < total)).astype(jnp.float32)


def on_device(design, flags, displacement, adjoint, pressure, multiplier):
    count_x, count_y, count_z = design.shape
    nodes = jnp.concatenate([displacement, adjoint], 0)
    arrived = from_behind(nodes[:, :1], "gx", -1)
    nodes = jnp.concatenate([nodes, arrived], 1)
    arrived = from_behind(nodes[:, :, :1], "gy", -1)
    nodes = jnp.concatenate([nodes, arrived], 2)
    arrived = from_behind(nodes[:, :, :, :1], "gz", -1)
    nodes = jnp.concatenate([nodes, arrived], 3)
    design_padded = with_halo(design, (("gx", 0), ("gy", 1), ("gz", 2)), 3)
    energy = element_energy(nodes[:3], nodes[3:], pressure, multiplier, count_x, count_y, count_z)
    inside_x = axis_inside(lax.axis_index("gx"), lax.axis_size("gx"), count_x)
    inside_y = axis_inside(lax.axis_index("gy"), lax.axis_size("gy"), count_y)
    inside_z = axis_inside(lax.axis_index("gz"), lax.axis_size("gz"), count_z)
    inside = inside_x[:, None, None] * inside_y[None, :, None] * inside_z[None, None, :]
    weight_total = cone_sum(inside, count_x, count_y, count_z)
    filtered = cone_sum(design_padded, count_x, count_y, count_z) / weight_total
    chain = projection(filtered, flags, energy, weight_total)
    chain_padded = with_halo(chain, (("gx", 0), ("gy", 1), ("gz", 2)), 3)
    summed = cone_sum(chain_padded, count_x, count_y, count_z)
    return jnp.where(flags >= 2, summed, 0.0)


def solution(mesh):
    in_specs = (
        P("gx", "gy", "gz"),
        P("gx", "gy", "gz"),
        P(None, "gx", "gy", "gz"),
        P(None, "gx", "gy", "gz"),
        P("gx", "gy", "gz"),
        P("gx", "gy", "gz"),
    )
    out_specs = P("gx", "gy", "gz")
    return jax.shard_map(
        on_device, mesh=mesh, in_specs=in_specs, out_specs=out_specs, check_vma=False
    )
```

profile of v0, /device:TPU:249, one launch (start us, length us, event | category | flops | bytes accessed | tf_op | source)
XLA Modules:
  0.0 137.0 jit_solution(2551197451076082007)
XLA Ops:
  0.0 1.1 copy.11
  1.1 1.1 copy.9
  2.2 6.6 %collective-permute-start.6 = (f32[6,1,8,256]{3,0,2,1:T(8,128)S(1)}, f32[6,1,8,256]{3,0,2,1:T(8,128)S(1)}, u32[]{:S(2)}, u32[]{:S(2)}) collective-permute-start(f32[6,1,8,256]{3,0,2,1:T(8,128)S(1)} %pad_maximum_fusion.13), channel_id=1, source_target_pairs={{64,0},{128,64},{192,128},{256,192},{320,256},{384,320},{448,384},... | collective-permute-start | bytes 147464 | tf_op jit(solution)/shard_map/ppermute | solution.py:19
  9.6 1.9 %collective-permute-start = (f32[3,8,256]{2,1,0:T(8,128)S(1)}, f32[3,8,256]{2,1,0:T(8,128)S(1)}, u32[]{:S(2)}, u32[]{:S(2)}) collective-permute-start(f32[3,8,256]{2,1,0:T(8,128)S(1)} %get-tuple-element.37), channel_id=1, source_target_pairs={{0,64},{64,128},{128,192},{192,256},{256,320},{320,384},{384,448},... | collective-permute-start | bytes 73736 | tf_op jit(solution)/shard_map/ppermute | solution.py:30
  11.5 9.4 %collective-permute-start.1 = (f32[3,8,256]{2,1,0:T(8,128)S(1)}, f32[3,8,256]{2,1,0:T(8,128)S(1)}, u32[]{:S(2)}, u32[]{:S(2)}) collective-permute-start(f32[3,8,256]{2,1,0:T(8,128)S(1)} %get-tuple-element.36), channel_id=1, source_target_pairs={{64,0},{128,64},{192,128},{256,192},{320,256},{384,320},{448,384},... | collective-permute-start | bytes 73736 | tf_op jit(solution)/shard_map/ppermute | solution.py:32
  21.1 3.7 %fusion.420 = f32[8,8,256]{2,1,0:T(8,128)} fusion(f32[14,14,262]{2,1,0:T(8,128)S(1)} %broadcast_multiply_fusion), kind=kLoop, calls=%fused_computation.677 | loop fusion | flops 5849088 | bytes 11796480 | tf_op jit(solution)/shard_map/add | solution.py:102
  24.9 2.1 %collective-permute-start.3 = (f32[14,3,256]{2,1,0:T(4,128)S(1)}, f32[14,3,256]{2,1,0:T(4,128)S(1)}, u32[]{:S(2)}, u32[]{:S(2)}) collective-permute-start(f32[14,3,256]{2,1,0:T(4,128)S(1)} %get-tuple-element.30), channel_id=1, source_target_pairs={{16,0},{32,16},{48,32},{17,1},{33,17},{49,33},{18,2},{34,18},{50,3... | collective-permute-start | bytes 129032 | tf_op jit(solution)/shard_map/ppermute | solution.py:32
  26.9 1.3 collective-permute-start.2
  29.2 4.0 %collective-permute-start.7 = (f32[6,9,1,256]{3,0,2,1:T(8,128)S(1)}, f32[6,9,1,256]{3,0,2,1:T(8,128)S(1)}, u32[]{:S(2)}, u32[]{:S(2)}) collective-permute-start(f32[6,9,1,256]{3,0,2,1:T(8,128)S(1)} %pad_maximum_fusion.10), channel_id=1, source_target_pairs={{16,0},{32,16},{48,32},{17,1},{33,17},{49,33},{18,2},{34,18},{50,3... | collective-permute-start | bytes 165896 | tf_op jit(solution)/shard_map/ppermute | solution.py:19
  33.4 7.5 %collective-permute-start.4 = (f32[14,14,3]{2,1,0:T(8,128)S(1)}, f32[14,14,3]{2,1,0:T(8,128)S(1)}, u32[]{:S(2)}, u32[]{:S(2)}) collective-permute-start(f32[14,14,3]{2,1,0:T(8,128)S(1)} %get-tuple-element.23), channel_id=1, source_target_pairs={{0,1},{1,2},{2,3},{3,4},{4,5},{5,6},{6,7},{7,8},{8,9},{9,10},{10,1... | collective-permute-start | bytes 7064 | tf_op jit(solution)/shard_map/ppermute | solution.py:30
  40.8 1.9 %collective-permute-start.5 = (f32[14,14,3]{2,1,0:T(8,128)S(1)}, f32[14,14,3]{2,1,0:T(8,128)S(1)}, u32[]{:S(2)}, u32[]{:S(2)}) collective-permute-start(f32[14,14,3]{2,1,0:T(8,128)S(1)} %get-tuple-element.24), channel_id=1, source_target_pairs={{1,0},{2,1},{3,2},{4,3},{5,4},{6,5},{7,6},{8,7},{9,8},{10,9},{11,1... | collective-permute-start | bytes 7064 | tf_op jit(solution)/shard_map/ppermute | solution.py:32
  43.6 4.6 %collective-permute-done.5 = f32[14,14,3]{2,1,0:T(8,128)S(1)} collective-permute-done((f32[14,14,3]{2,1,0:T(8,128)S(1)}, f32[14,14,3]{2,1,0:T(8,128)S(1)}, u32[]{:S(2)}, u32[]{:S(2)}) %collective-permute-start.5) | collective-permute-done | bytes 2384 | tf_op jit(solution)/shard_map/ppermute | solution.py:32
  48.6 1.9 %collective-permute-start.8 = (f32[6,9,9,1]{3,0,2,1:T(8,128)S(1)}, f32[6,9,9,1]{3,0,2,1:T(8,128)S(1)}, u32[]{:S(2)}, u32[]{:S(2)}) collective-permute-start(f32[6,9,9,1]{3,0,2,1:T(8,128)S(1)} %slice.3036), channel_id=1, source_target_pairs={{1,0},{2,1},{3,2},{4,3},{5,4},{6,5},{7,6},{8,7},{9,8},{10,9},{11,1... | collective-permute-start | bytes 5840 | tf_op jit(solution)/shard_map/ppermute | solution.py:19
  50.5 1.1 fusion.616
  51.6 6.6 %collective-permute-done.8 = f32[6,9,9,1]{3,0,2,1:T(8,128)S(1)} collective-permute-done((f32[6,9,9,1]{3,0,2,1:T(8,128)S(1)}, f32[6,9,9,1]{3,0,2,1:T(8,128)S(1)}, u32[]{:S(2)}, u32[]{:S(2)}) %collective-permute-start.8) | collective-permute-done | bytes 1976 | tf_op jit(solution)/shard_map/ppermute | solution.py:19
  58.4 2.3 %fusion.615 = (f32[3,8,8,256]{3,0,2,1:T(4,128)}, f32[3,8,8,256]{3,0,2,1:T(4,128)}, f32[3,8,8,256]{3,0,2,1:T(4,128)}, f32[3,8,8,256]{3,0,2,1:T(4,128)}, f32[3,8,8...) fusion(f32[6,9,9,257]{3,0,2,1:T(8,128)S(1)} %pad_maximum_fusion), kind=kLoop, calls=%fused_computation.1214 | loop fusion | bytes 3145728 | tf_op jit(solution)/shard_map/slice | solution.py:116
  60.7 11.4 %concatenate.425 = f32[24,8,8,256]{3,0,2,1:T(8,128)S(1)} concatenate(f32[3,8,8,256]{3,0,2,1:T(4,128)S(1)} %copy.9, f32[3,8,8,256]{3,0,2,1:T(4,128)} %pad_maximum_fusion.5, f32[3,8,8,256]{3,0,2,1:T(4,128)} %get-tuple-element.14, f32[3,8,8,256]{3,0,2,1:T(4,128)} %get-tuple-element.13, f32[3,8,8,256]{3,0,2,1:T(4,128)} %get-tuple-element.8, f32[3,8,8,256]{3,0,2,1:T(4,128)} %get-tuple-element.7, ...), dimensions={0} | concatenate | bytes 3145728 | tf_op jit(solution)/shard_map/concatenate | solution.py:118
  72.1 0.9 fusion.624
  73.0 16.7 %concatenate.424 = f32[24,8,8,256]{3,0,2,1:T(8,128)} concatenate(f32[3,8,8,256]{3,0,2,1:T(4,128)S(1)} %copy.11, f32[3,8,8,256]{3,0,2,1:T(4,128)} %slice.3033, f32[3,8,8,256]{3,0,2,1:T(4,128)} %get-tuple-element.16, f32[3,8,8,256]{3,0,2,1:T(4,128)} %get-tuple-element.15, f32[3,8,8,256]{3,0,2,1:T(4,128)} %get-tuple-element.12, f32[3,8,8,256]{3,0,2,1:T(4,128)S(1)} %copy-done.1, ...), dimensions={0} | concatenate | bytes 3145728 | tf_op jit(solution)/shard_map/concatenate | solution.py:118
  89.7 2.5 %fusion.623 = f32[1,8,8,256]{3,0,2,1:T(1,128)S(1)} fusion(f32[24,8,8,256]{3,0,2,1:T(8,128)} %concatenate.424, f32[24,1,1,1]{0,1,3,2:T(1,128)S(1)} %copy-done.15), kind=kOutput, calls=%fused_computation.1222 | convolution fusion | flops 4718592 | bytes 1638496 | tf_op jit(solution)/shard_map/j,jxyz->xyz/dot_general | solution.py:126
  92.3 1.5 %multiply_reduce_fusion = f32[8,8,256]{2,1,0:T(8,128)S(1)} fusion(f32[24,8,8,256]{3,0,2,1:T(8,128)S(1)} %copy-done, f32[24,24,1,1]{1,0,3,2:T(8,128)S(1)} %copy-done.14, f32[24,8,8,256]{3,0,2,1:T(8,128)S(1)} %concatenate.425), kind=kOutput, calls=%fused_computation | convolution fusion | flops 114016256 | bytes 3213568 | tf_op jit(solution)/shard_map/ij,jxyz->ixyz/dot_general | solution.py:122
  93.9 2.5 %fusion.91 = f32[8,8,256]{2,1,0:T(8,128)S(1)} fusion(f32[8,8,256]{2,1,0:T(8,128)S(1)} %copy-done.11, f32[8,8,256]{2,1,0:T(8,128)S(1)} %copy-done.12, f32[8,8,256]{2,1,0:T(8,128)S(1)} %multiply_reduce_fusion, f32[8,8,256]{2,1,0:T(8,128)S(1)} %copy-done.13, f32[1,8,8,256]{3,0,2,1:T(1,128)S(1)} %fusion.624, f32[1,8,8,256]{3,0,2,1:T(1,128)S(1)} %fusion.623, ...), kind=kLoop, calls=%fused_computation.172 | loop fusion | flops 6766592 | bytes 10489856 | tf_op jit(solution)/shard_map/div | solution.py:143
  96.5 7.5 %collective-permute-start.10 = (f32[3,8,256]{2,1,0:T(8,128)S(1)}, f32[3,8,256]{2,1,0:T(8,128)S(1)}, u32[]{:S(2)}, u32[]{:S(2)}) collective-permute-start(f32[3,8,256]{2,1,0:T(8,128)S(1)} %get-tuple-element.32), channel_id=1, source_target_pairs={{64,0},{128,64},{192,128},{256,192},{320,256},{384,320},{448,384},... | collective-permute-start | bytes 73736 | tf_op jit(solution)/shard_map/ppermute | solution.py:32
  104.0 1.9 %collective-permute-start.9 = (f32[3,8,256]{2,1,0:T(8,128)S(1)}, f32[3,8,256]{2,1,0:T(8,128)S(1)}, u32[]{:S(2)}, u32[]{:S(2)}) collective-permute-start(f32[3,8,256]{2,1,0:T(8,128)S(1)} %get-tuple-element.31), channel_id=1, source_target_pairs={{0,64},{64,128},{128,192},{192,256},{256,320},{320,384},{384,448},... | collective-permute-start | bytes 73736 | tf_op jit(solution)/shard_map/ppermute | solution.py:30
  105.9 8.6 %collective-permute-done.9 = f32[3,8,256]{2,1,0:T(8,128)S(1)} collective-permute-done((f32[3,8,256]{2,1,0:T(8,128)S(1)}, f32[3,8,256]{2,1,0:T(8,128)S(1)}, u32[]{:S(2)}, u32[]{:S(2)}) %collective-permute-start.9) | collective-permute-done | bytes 24608 | tf_op jit(solution)/shard_map/ppermute | solution.py:30
  114.6 2.0 %collective-permute-start.12 = (f32[14,3,256]{2,1,0:T(4,128)S(1)}, f32[14,3,256]{2,1,0:T(4,128)S(1)}, u32[]{:S(2)}, u32[]{:S(2)}) collective-permute-start(f32[14,3,256]{2,1,0:T(4,128)S(1)} %get-tuple-element.28), channel_id=1, source_target_pairs={{16,0},{32,16},{48,32},{17,1},{33,17},{49,33},{18,2},{34,18},{50,3... | collective-permute-start | bytes 129032 | tf_op jit(solution)/shard_map/ppermute | solution.py:32
  116.7 1.3 collective-permute-start.11
  118.0 3.6 %collective-permute-done.11 = f32[14,3,256]{2,1,0:T(4,128)S(1)} collective-permute-done((f32[14,3,256]{2,1,0:T(4,128)S(1)}, f32[14,3,256]{2,1,0:T(4,128)S(1)}, u32[]{:S(2)}, u32[]{:S(2)}) %collective-permute-start.11) | collective-permute-done | bytes 43040 | tf_op jit(solution)/shard_map/ppermute | solution.py:30
  121.7 4.6 %collective-permute-start.13 = (f32[14,14,3]{2,1,0:T(8,128)S(1)}, f32[14,14,3]{2,1,0:T(8,128)S(1)}, u32[]{:S(2)}, u32[]{:S(2)}) collective-permute-start(f32[14,14,3]{2,1,0:T(8,128)S(1)} %get-tuple-element.19), channel_id=1, source_target_pairs={{0,1},{1,2},{2,3},{3,4},{4,5},{5,6},{6,7},{7,8},{8,9},{9,10},{10,1... | collective-permute-start | bytes 7064 | tf_op jit(solution)/shard_map/ppermute | solution.py:30
  126.3 1.9 %collective-permute-start.14 = (f32[14,14,3]{2,1,0:T(8,128)S(1)}, f32[14,14,3]{2,1,0:T(8,128)S(1)}, u32[]{:S(2)}, u32[]{:S(2)}) collective-permute-start(f32[14,14,3]{2,1,0:T(8,128)S(1)} %get-tuple-element.20), channel_id=1, source_target_pairs={{1,0},{2,1},{3,2},{4,3},{5,4},{6,5},{7,6},{8,7},{9,8},{10,9},{11,1... | collective-permute-start | bytes 7064 | tf_op jit(solution)/shard_map/ppermute | solution.py:32
  128.3 5.3 %collective-permute-done.14 = f32[14,14,3]{2,1,0:T(8,128)S(1)} collective-permute-done((f32[14,14,3]{2,1,0:T(8,128)S(1)}, f32[14,14,3]{2,1,0:T(8,128)S(1)}, u32[]{:S(2)}, u32[]{:S(2)}) %collective-permute-start.14) | collective-permute-done | bytes 2384 | tf_op jit(solution)/shard_map/ppermute | solution.py:32
  133.9 3.1 %fusion.320 = f32[8,8,256]{2,1,0:T(8,128)} fusion(f32[14,14,259]{2,1,0:T(8,128)S(1)} %get-tuple-element.18, f32[14,11,256]{2,1,0:T(8,128)S(1)} %get-tuple-element.26, f32[14,14,259]{2,1,0:T(8,128)S(1)} %get-tuple-element.17, f32[3,8,256]{2,1,0:T(8,128)S(1)} %collective-permute-done.10, f32[8,8,256]{2,1,0:T(8,128)S(1)} %fusion.91, ...), kind=kLoop, calls=%fused_computation.402 | loop fusion | flops 5980160 | bytes 11517952 | tf_op jit(solution)/shard_map/jit(_where)/select_n | solution.py:172
  (69 shorter events, 4.0 us)
Async XLA Ops:
  2.2 26.1 %collective-permute-start.6 = (f32[6,1,8,256]{3,0,2,1:T(8,128)S(1)}, f32[6,1,8,256]{3,0,2,1:T(8,128)S(1)}, u32[]{:S(2)}, u32[]{:S(2)}) collective-permute-start(f32[6,1,8,256]{3,0,2,1:T(8,128)S(1)} %pad_maximum_fusion.13), channel_id=1, source_target_pairs={{64,0},{128,64},{192,128},{256,192},{320,256},{384,320},{448,384},... | collective-permute-start | bytes 147464 | tf_op jit(solution)/shard_map/ppermute | solution.py:19
  9.6 15.2 %collective-permute-start = (f32[3,8,256]{2,1,0:T(8,128)S(1)}, f32[3,8,256]{2,1,0:T(8,128)S(1)}, u32[]{:S(2)}, u32[]{:S(2)}) collective-permute-start(f32[3,8,256]{2,1,0:T(8,128)S(1)} %get-tuple-element.37), channel_id=1, source_target_pairs={{0,64},{64,128},{128,192},{192,256},{256,320},{320,384},{384,448},... | collective-permute-start | bytes 73736 | tf_op jit(solution)/shard_map/ppermute | solution.py:30
  11.5 13.3 %collective-permute-start.1 = (f32[3,8,256]{2,1,0:T(8,128)S(1)}, f32[3,8,256]{2,1,0:T(8,128)S(1)}, u32[]{:S(2)}, u32[]{:S(2)}) collective-permute-start(f32[3,8,256]{2,1,0:T(8,128)S(1)} %get-tuple-element.36), channel_id=1, source_target_pairs={{64,0},{128,64},{192,128},{256,192},{320,256},{384,320},{448,384},... | collective-permute-start | bytes 73736 | tf_op jit(solution)/shard_map/ppermute | solution.py:32
  21.1 3.7 %copy-start.8 = (f32[8,8,256]{2,1,0:T(8,128)S(1)}, f32[8,8,256]{2,1,0:T(8,128)}, u32[]{:S(2)}) copy-start(f32[8,8,256]{2,1,0:T(8,128)} %param.8) | copy-start | bytes 196612
  24.8 3.5 %copy-start.4 = (f32[11,8,256]{2,1,0:T(8,128)}, f32[11,8,256]{2,1,0:T(8,128)S(1)}, u32[]{:S(2)}) copy-start(f32[11,8,256]{2,1,0:T(8,128)S(1)} %get-tuple-element.33) | copy-start | bytes 270340
  24.8 3.4 %copy-start.2 = (f32[11,8,256]{2,1,0:T(8,128)}, f32[11,8,256]{2,1,0:T(8,128)S(1)}, u32[]{:S(2)}) copy-start(f32[11,8,256]{2,1,0:T(8,128)S(1)} %get-tuple-element.40) | copy-start | bytes 270340
  24.9 8.3 %collective-permute-start.3 = (f32[14,3,256]{2,1,0:T(4,128)S(1)}, f32[14,3,256]{2,1,0:T(4,128)S(1)}, u32[]{:S(2)}, u32[]{:S(2)}) collective-permute-start(f32[14,3,256]{2,1,0:T(4,128)S(1)} %get-tuple-element.30), channel_id=1, source_target_pairs={{16,0},{32,16},{48,32},{17,1},{33,17},{49,33},{18,2},{34,18},{50,3... | collective-permute-start | bytes 129032 | tf_op jit(solution)/shard_map/ppermute | solution.py:32
  26.9 6.2 %collective-permute-start.2 = (f32[14,3,256]{2,1,0:T(4,128)S(1)}, f32[14,3,256]{2,1,0:T(4,128)S(1)}, u32[]{:S(2)}, u32[]{:S(2)}) collective-permute-start(f32[14,3,256]{2,1,0:T(4,128)S(1)} %get-tuple-element.29), channel_id=1, source_target_pairs={{0,16},{16,32},{32,48},{1,17},{17,33},{33,49},{2,18},{18,34},{34,5... | collective-permute-start | bytes 129032 | tf_op jit(solution)/shard_map/ppermute | solution.py:30
  29.2 19.2 %collective-permute-start.7 = (f32[6,9,1,256]{3,0,2,1:T(8,128)S(1)}, f32[6,9,1,256]{3,0,2,1:T(8,128)S(1)}, u32[]{:S(2)}, u32[]{:S(2)}) collective-permute-start(f32[6,9,1,256]{3,0,2,1:T(8,128)S(1)} %pad_maximum_fusion.10), channel_id=1, source_target_pairs={{16,0},{32,16},{48,32},{17,1},{33,17},{49,33},{18,2},{34,18},{50,3... | collective-permute-start | bytes 165896 | tf_op jit(solution)/shard_map/ppermute | solution.py:19
  33.2 15.3 %copy-start.6 = (f32[14,3,256]{2,1,0:T(4,128)}, f32[14,3,256]{2,1,0:T(4,128)S(1)}, u32[]{:S(2)}) copy-start(f32[14,3,256]{2,1,0:T(4,128)S(1)} %collective-permute-done.2) | copy-start | bytes 129028
  33.4 10.2 %collective-permute-start.4 = (f32[14,14,3]{2,1,0:T(8,128)S(1)}, f32[14,14,3]{2,1,0:T(8,128)S(1)}, u32[]{:S(2)}, u32[]{:S(2)}) collective-permute-start(f32[14,14,3]{2,1,0:T(8,128)S(1)} %get-tuple-element.23), channel_id=1, source_target_pairs={{0,1},{1,2},{2,3},{3,4},{4,5},{5,6},{6,7},{7,8},{8,9},{9,10},{10,1... | collective-permute-start | bytes 7064 | tf_op jit(solution)/shard_map/ppermute | solution.py:30
  40.8 7.3 %collective-permute-start.5 = (f32[14,14,3]{2,1,0:T(8,128)S(1)}, f32[14,14,3]{2,1,0:T(8,128)S(1)}, u32[]{:S(2)}, u32[]{:S(2)}) collective-permute-start(f32[14,14,3]{2,1,0:T(8,128)S(1)} %get-tuple-element.24), channel_id=1, source_target_pairs={{1,0},{2,1},{3,2},{4,3},{5,4},{6,5},{7,6},{8,7},{9,8},{10,9},{11,1... | collective-permute-start | bytes 7064 | tf_op jit(solution)/shard_map/ppermute | solution.py:32
  48.6 9.6 %collective-permute-start.8 = (f32[6,9,9,1]{3,0,2,1:T(8,128)S(1)}, f32[6,9,9,1]{3,0,2,1:T(8,128)S(1)}, u32[]{:S(2)}, u32[]{:S(2)}) collective-permute-start(f32[6,9,9,1]{3,0,2,1:T(8,128)S(1)} %slice.3036), channel_id=1, source_target_pairs={{1,0},{2,1},{3,2},{4,3},{5,4},{6,5},{7,6},{8,7},{9,8},{10,9},{11,1... | collective-permute-start | bytes 5840 | tf_op jit(solution)/shard_map/ppermute | solution.py:19
  60.7 11.4 %copy-start.15 = (f32[24,1,1,1]{0,1,3,2:T(1,128)S(1)}, f32[24,1,1,1]{0,1,3,2:T(1,128)}, u32[]{:S(2)}) copy-start(f32[24,1,1,1]{0,1,3,2:T(1,128)} %constant.92) | copy-start | bytes 292
  72.0 1.0 copy-start.1
  89.6 2.5 %copy-start = (f32[24,8,8,256]{3,0,2,1:T(8,128)S(1)}, f32[24,8,8,256]{3,0,2,1:T(8,128)}, u32[]{:S(2)}) copy-start(f32[24,8,8,256]{3,0,2,1:T(8,128)} %concatenate.424) | copy-start | bytes 4718596
  89.6 2.5 %copy-start.14 = (f32[24,24,1,1]{1,0,3,2:T(8,128)S(1)}, f32[24,24,1,1]{1,0,3,2:T(8,128)}, u32[]{:S(2)}) copy-start(f32[24,24,1,1]{1,0,3,2:T(8,128)} %constant.91) | copy-start | bytes 6916
  92.2 1.6 %copy-start.3 = (f32[11,8,256]{2,1,0:T(8,128)S(1)}, f32[11,8,256]{2,1,0:T(8,128)}, u32[]{:S(2)}) copy-start(f32[11,8,256]{2,1,0:T(8,128)} %copy-done.2) | copy-start | bytes 270340
  92.2 1.6 %copy-start.5 = (f32[11,8,256]{2,1,0:T(8,128)S(1)}, f32[11,8,256]{2,1,0:T(8,128)}, u32[]{:S(2)}) copy-start(f32[11,8,256]{2,1,0:T(8,128)} %copy-done.4) | copy-start | bytes 270340
  92.2 1.6 %copy-start.7 = (f32[14,3,256]{2,1,0:T(4,128)S(1)}, f32[14,3,256]{2,1,0:T(4,128)}, u32[]{:S(2)}) copy-start(f32[14,3,256]{2,1,0:T(4,128)} %copy-done.6) | copy-start | bytes 129028
  92.2 1.6 %copy-start.9 = (f32[8,8,256]{2,1,0:T(8,128)S(1)}, f32[8,8,256]{2,1,0:T(8,128)}, u32[]{:S(2)}) copy-start(f32[8,8,256]{2,1,0:T(8,128)} %param.8) | copy-start | bytes 196612
  92.2 1.6 %copy-start.10 = (s32[8,8,256]{2,1,0:T(8,128)S(1)}, s32[8,8,256]{2,1,0:T(8,128)}, u32[]{:S(2)}) copy-start(s32[8,8,256]{2,1,0:T(8,128)} %param.9) | copy-start | bytes 196612
  92.2 1.6 %copy-start.11 = (f32[8,8,256]{2,1,0:T(8,128)S(1)}, f32[8,8,256]{2,1,0:T(8,128)}, u32[]{:S(2)}) copy-start(f32[8,8,256]{2,1,0:T(8,128)} %fusion.420) | copy-start | bytes 196612
  92.3 1.6 %copy-start.12 = (f32[8,8,256]{2,1,0:T(8,128)S(1)}, f32[8,8,256]{2,1,0:T(8,128)}, u32[]{:S(2)}) copy-start(f32[8,8,256]{2,1,0:T(8,128)} %param.13) | copy-start | bytes 196612
  92.3 1.6 %copy-start.13 = (f32[8,8,256]{2,1,0:T(8,128)S(1)}, f32[8,8,256]{2,1,0:T(8,128)}, u32[]{:S(2)}) copy-start(f32[8,8,256]{2,1,0:T(8,128)} %param.12) | copy-start | bytes 196612
  96.5 9.5 %collective-permute-start.10 = (f32[3,8,256]{2,1,0:T(8,128)S(1)}, f32[3,8,256]{2,1,0:T(8,128)S(1)}, u32[]{:S(2)}, u32[]{:S(2)}) collective-permute-start(f32[3,8,256]{2,1,0:T(8,128)S(1)} %get-tuple-element.32), channel_id=1, source_target_pairs={{64,0},{128,64},{192,128},{256,192},{320,256},{384,320},{448,384},... | collective-permute-start | bytes 73736 | tf_op jit(solution)/shard_map/ppermute | solution.py:32
  104.0 10.6 %collective-permute-start.9 = (f32[3,8,256]{2,1,0:T(8,128)S(1)}, f32[3,8,256]{2,1,0:T(8,128)S(1)}, u32[]{:S(2)}, u32[]{:S(2)}) collective-permute-start(f32[3,8,256]{2,1,0:T(8,128)S(1)} %get-tuple-element.31), channel_id=1, source_target_pairs={{0,64},{64,128},{128,192},{192,256},{256,320},{320,384},{384,448},... | collective-permute-start | bytes 73736 | tf_op jit(solution)/shard_map/ppermute | solution.py:30
  114.6 3.4 %collective-permute-start.12 = (f32[14,3,256]{2,1,0:T(4,128)S(1)}, f32[14,3,256]{2,1,0:T(4,128)S(1)}, u32[]{:S(2)}, u32[]{:S(2)}) collective-permute-start(f32[14,3,256]{2,1,0:T(4,128)S(1)} %get-tuple-element.28), channel_id=1, source_target_pairs={{16,0},{32,16},{48,32},{17,1},{33,17},{49,33},{18,2},{34,18},{50,3... | collective-permute-start | bytes 129032 | tf_op jit(solution)/shard_map/ppermute | solution.py:32
  116.7 4.9 %collective-permute-start.11 = (f32[14,3,256]{2,1,0:T(4,128)S(1)}, f32[14,3,256]{2,1,0:T(4,128)S(1)}, u32[]{:S(2)}, u32[]{:S(2)}) collective-permute-start(f32[14,3,256]{2,1,0:T(4,128)S(1)} %get-tuple-element.27), channel_id=1, source_target_pairs={{0,16},{16,32},{32,48},{1,17},{17,33},{33,49},{2,18},{18,34},{34,5... | collective-permute-start | bytes 129032 | tf_op jit(solution)/shard_map/ppermute | solution.py:30
  121.7 6.6 %collective-permute-start.13 = (f32[14,14,3]{2,1,0:T(8,128)S(1)}, f32[14,14,3]{2,1,0:T(8,128)S(1)}, u32[]{:S(2)}, u32[]{:S(2)}) collective-permute-start(f32[14,14,3]{2,1,0:T(8,128)S(1)} %get-tuple-element.19), channel_id=1, source_target_pairs={{0,1},{1,2},{2,3},{3,4},{4,5},{5,6},{6,7},{7,8},{8,9},{9,10},{10,1... | collective-permute-start | bytes 7064 | tf_op jit(solution)/shard_map/ppermute | solution.py:30
  126.3 7.3 %collective-permute-start.14 = (f32[14,14,3]{2,1,0:T(8,128)S(1)}, f32[14,14,3]{2,1,0:T(8,128)S(1)}, u32[]{:S(2)}, u32[]{:S(2)}) collective-permute-start(f32[14,14,3]{2,1,0:T(8,128)S(1)} %get-tuple-element.20), channel_id=1, source_target_pairs={{1,0},{2,1},{3,2},{4,3},{5,4},{6,5},{7,6},{8,7},{9,8},{10,9},{11,1... | collective-permute-start | bytes 7064 | tf_op jit(solution)/shard_map/ppermute | solution.py:32
where the time goes:
time: 138 us; the launch traced here: 137 us
  starting transfers between devices  55.9 us (41%)
  local copies, waits for them, and re-layouts  35.4 us (26%)
  waiting for transfers between devices  28.8 us (21%)
  other arithmetic  11.4 us (8%)
  matrix products  4.96 us (4%)
    concatenate x2, local copies, waits for them, and re-layouts, gather_dofs(): return jnp.concatenate(pieces, 0)  28 us
    ppermute x6, starting transfers between devices, with_halo(): lax.ppermute(head, axis, [((i + 1) % count, i) for i in range(ends)])  24.9 us
    ppermute x6, starting transfers between devices, with_halo(): lax.ppermute(tail, axis, [(i, (i + 1) % count) for i in range(ends)])  18.5 us
    ppermute x3, starting transfers between devices, from_behind(): return lax.ppermute(value, axis, pairs)  12.5 us
    ppermute x6, waiting for transfers between devices, with_halo(): lax.ppermute(tail, axis, [(i, (i + 1) % count) for i in range(ends)])  12.3 us
    ppermute x6, waiting for transfers between devices, with_halo(): lax.ppermute(head, axis, [((i + 1) % count, i) for i in range(ends)])  9.91 us
    ppermute x3, waiting for transfers between devices, from_behind(): return lax.ppermute(value, axis, pairs)  6.61 us
    slice x3, local copies, waits for them, and re-layouts, gather_dofs(): field[:, bit_x:bit_x + count_x, bit_y:bit_y + count_y, bit_z:bit_z + coun...  4.16 us
  transfers between devices with their start and end apart: 15, of which 5 were waited for; matrix products, arithmetic and copies ran while one was open for 6% of the time, Pallas kernels for 0%

commit v1 on v0

v1 whole, which is shorter than its diff:
```python
import functools
import itertools
import math

import jax
import jax.numpy as jnp
from jax import lax
from jax.experimental import pallas as pl
from jax.experimental.pallas import tpu as pltpu
from jax.sharding import PartitionSpec as P

poisson = 0.45
sharpness = 4.0
threshold = 0.5
stiff_floor = 0.001
cone_radius = 3.5

AXES = ("gx", "gy", "gz")
NX, NY, NZ = 8, 8, 256
MESH = pl.DeviceIdType.MESH
OFFSETS = sorted(
    (o for o in itertools.product((-1, 0, 1), repeat=3) if any(o)), key=lambda o: (-abs(o[0]), o)
)


def cone_weight(a, b, c):
    r2 = a * a + b * b + c * c
    return cone_radius - math.sqrt(r2) if r2 < cone_radius * cone_radius else 0.0


def place(grid):
    return [lax.axis_index(a) for a in AXES]


def peer(grid, offset):
    at = [lax.axis_index(a) for a in AXES]
    target = tuple(a + o for a, o in zip(at, offset))
    ok = None
    for t, o, n in zip(target, offset, grid):
        if o:
            inside = t >= 0 if o < 0 else t < n
            ok = inside if ok is None else ok & inside
    return target, ok


def opposite(offset):
    return tuple(-o for o in offset)


class Exchange:
    def __init__(self, grid, send, recv):
        self.grid, self.send, self.recv = grid, send, recv
        self.items = []

    def copy(self, index):
        offset, src, dst = self.items[index]
        target, ok = peer(self.grid, offset)
        return ok, pltpu.make_async_remote_copy(
            src_ref=src, dst_ref=dst, send_sem=self.send.at[index], recv_sem=self.recv.at[index],
            device_id=target, device_id_type=MESH,
        )

    def start(self, offset, src, dst):
        self.items.append((offset, src, dst))
        ok, copy = self.copy(len(self.items) - 1)
        pl.when(ok)(copy.start)

    def finish_recv(self, index):
        offset, src, dst = self.items[index]
        _, ok = peer(self.grid, opposite(offset))
        _, copy = self.copy(index)
        pl.when(ok)(copy.wait_recv)

        @pl.when(jnp.logical_not(ok))
        def _():
            dst[...] = jnp.zeros(dst.shape, jnp.float32)

    def finish_send(self, index):
        ok, copy = self.copy(index)
        pl.when(ok)(copy.wait_send)


def roll(value, by, axis):
    by = by % value.shape[axis]
    return value if by == 0 else pltpu.roll(value, by, axis)


def iota(shape, dim):
    return lax.broadcasted_iota(jnp.int32, shape, dim)


def cone_sum(vol, ysum, emit):
    row = iota((2, 8, 384), 1)

    def rows(p, _):
        at = pl.ds(2 * p, 2)
        low, high = vol[at, 0:8, :], vol[at, 8:16, :]
        for b in (1, 2, 3):
            up = roll(jnp.where(row < b, high, low), -b, 1)
            down = roll(jnp.where(row >= 8 - b, high, low), b, 1)
            ysum[b - 1, at] = up + down
        return 0

    lax.fori_loop(0, 7, rows, 0)
    lane = iota((2, 8, 128), 2)

    def planes(p, _):
        x = 2 * p
        sums = {}

        def get(b, k):
            return vol[pl.ds(x + k, 2), 0:8, :] if b == 0 else ysum[b - 1, pl.ds(x + k, 2)]

        for a in range(4):
            for b in range(4):
                if a * a + b * b < 12.25:
                    sums[a, b] = get(b, 3) if a == 0 else get(b, 3 - a) + get(b, 3 + a)
        groups = {}
        for (a, b), value in sums.items():
            key = (min(a, b), max(a, b))
            groups[key] = groups[key] + value if key in groups else value
        total = None
        for c in range(4):
            g = None
            for (a, b), value in groups.items():
                w = cone_weight(a, b, c)
                if w > 0:
                    g = value * w if g is None else g + value * w
            g0, g1, gh = g[:, :, 0:128], g[:, :, 128:256], g[:, :, 256:384]
            if c == 0:
                t0, t1 = g0, g1
            else:
                t0 = t0 + roll(jnp.where(lane < c, g1, g0), -c, 2) + roll(
                    jnp.where(lane >= 128 - c, gh, g0), c, 2)
                t1 = t1 + roll(jnp.where(lane < c, gh, g1), -c, 2) + roll(
                    jnp.where(lane >= 128 - c, g0, g1), c, 2)
        emit(x, t0, t1)
        return 0

    lax.fori_loop(0, 4, planes, 0)


def inverse_weight(grid, out):
    gx, gy, gz = [lax.axis_index(a) for a in AXES]
    y = gy * NY + iota((NY, NZ), 0)
    z = gz * NZ + iota((NY, NZ), 1)

    def pairs(pos, by, size):
        return (pos + by < size).astype(jnp.float32) + (pos - by >= 0).astype(jnp.float32)

    ys = [None] + [pairs(y, b, grid[1] * NY) for b in (1, 2, 3)]
    zs = [None] + [pairs(z, c, grid[2] * NZ) for c in (1, 2, 3)]
    fs = []
    for a in range(4):
        f = jnp.full((NY, NZ), 0.0, jnp.float32)
        for b in range(4):
            for c in range(4):
                w = cone_weight(a, b, c)
                if w > 0:
                    term = jnp.float32(w)
                    term = term if b == 0 else term * ys[b]
                    term = term if c == 0 else term * zs[c]
                    f = f + term
        fs.append(f)
    for x in range(NX):
        px = gx * NX + x
        w = fs[0]
        for a in (1, 2, 3):
            w = w + fs[a] * pairs(px, a, grid[0] * NX)
        out[x] = 1.0 / w


def assemble(vol, ybuf, edge, strip):
    row = iota((8, 256), 0)
    rowl = iota((8, 128), 0)
    lane = iota((8, 128), 1)
    for i in range(8):
        vol[3 + i, 8:16, 0:256] = jnp.where(row < 4, ybuf[0, i], ybuf[1, i])
    for k in range(3):
        vol[k, 8:16, 0:256] = jnp.where(row < 4, edge[0, 0, k], edge[0, 1, k])
        vol[11 + k, 8:16, 0:256] = jnp.where(row < 4, edge[1, 0, k], edge[1, 1, k])
    both = {}
    for dx in range(3):
        for dy in range(3):
            both[dx, dy] = jnp.where((lane & 15) < 12, strip[0, dx, dy], strip[1, dx, dy])
    for dx in range(3):
        main = both[dx, 1]
        side = jnp.where(rowl < 4, both[dx, 2], both[dx, 0])
        first, count, at = ((5, 3, 0), (0, 8, 3), (0, 3, 11))[dx]
        for k in range(count):
            vol[at + k, 0:8, 256:384] = roll(main, -16 * (first + k), 1)
            vol[at + k, 8:16, 256:384] = roll(side, -16 * (first + k), 1)
    return both


def send_volume(ex, vol, ybuf, edge, strip, pack):
    center = vol.at[pl.ds(3, 8), pl.ds(0, 8), pl.ds(0, 256)]
    low3 = vol.at[pl.ds(3, 3), pl.ds(0, 8), pl.ds(0, 256)]
    high3 = vol.at[pl.ds(8, 3), pl.ds(0, 8), pl.ds(0, 256)]
    for o in OFFSETS:
        dx, dy, dz = o
        if dz:
            ex.start(o, pack.at[0 if dz < 0 else 1], strip.at[0 if dz < 0 else 1, 1 - dx, 1 - dy])
        elif dx and dy:
            ex.start(o, low3 if dx < 0 else high3, edge.at[1 if dx < 0 else 0, 0 if dy < 0 else 1])
        elif dx:
            lands = pl.ds(11, 3) if dx < 0 else pl.ds(0, 3)
            ex.start(o, low3 if dx < 0 else high3, vol.at[lands, pl.ds(0, 8), pl.ds(0, 256)])
        else:
            ex.start(o, center, ybuf.at[0 if dy < 0 else 1])


def pack_strips(vol, pack, nodes):
    lane = iota((8, 128), 1)
    down, up = None, None
    for i in range(8):
        first, last = vol[3 + i, 0:8, 0:128], vol[3 + i, 0:8, 128:256]
        d, u = roll(first, 16 * i, 1), roll(last, 16 * i, 1)
        if i == 0:
            down, up = d, u
        else:
            down = jnp.where((lane >= 16 * i) & (lane < 16 * i + 3), d, down)
            up = jnp.where((lane >= 16 * i - 3) & (lane < 16 * i), u, up)
        if nodes is not None:
            for f in range(6):
                n = roll(nodes[f, i, :, 0:128], 16 * i + 3 + f, 1)
                down = jnp.where(lane == 16 * i + 3 + f, n, down)
    pack[0] = down
    pack[1] = up


def node_modes(nodes, rows, corner, both, modes):
    lane = iota((8, 128), 1)
    row = iota((8, 128), 0)
    for p in range(9):
        dx = 2 if p == 8 else 1
        base = 0 if p == 8 else 16 * p
        for f in range(6):
            n0, n1 = nodes[f, p, :, 0:128], nodes[f, p, :, 128:256]
            if p == 8:
                top = corner[f:f + 1, :]
            else:
                top = rows[f, p:p + 1, :]
            e0, e1 = top[:, 0:128], top[:, 128:256]
            h = roll(both[dx, 1], -(base + 3 + f), 1)
            eh = roll(both[dx, 2], -(base + 3 + f), 1)
            up = lambda v: roll(v, -1, 1)
            s0 = up(jnp.where(lane == 0, n1, n0))
            s1 = up(jnp.where(lane == 0, h, n1))
            m0 = roll(jnp.where(row == 0, jnp.broadcast_to(e0, (8, 128)), n0), -1, 0)
            m1 = roll(jnp.where(row == 0, jnp.broadcast_to(e1, (8, 128)), n1), -1, 0)
            mh = roll(jnp.where(row == 0, eh, h), -1, 0)
            q0 = up(jnp.where(lane == 0, m1, m0))
            q1 = up(jnp.where(lane == 0, mh, m1))
            for half, (n, s, m, q) in enumerate(((n0, s0, m0, q0), (n1, s1, m1, q1))):
                a, d = n + s, s - n
                ay, dy = m + q, q - m
                at = pl.ds(128 * half, 128)
                modes[p, f, 0, :, at] = a + ay
                modes[p, f, 1, :, at] = d + dy
                modes[p, f, 2, :, at] = ay - a
                modes[p, f, 3, :, at] = dy - d


def element_energy(modes, x, press, mult):
    shear = 1.0 / (2.0 * (1.0 + poisson))
    bulk = 1.0 / (3.0 * (1.0 - 2.0 * poisson))

    def both_of(f, m):
        return modes[x, f, m], modes[x + 1, f, m]

    def field(base):
        out = []
        for c in range(3):
            aa, ad, da, dd = (both_of(base + c, m) for m in range(4))
            out.append(dict(
                X=aa[1] - aa[0], Y=da[0] + da[1], Z=ad[0] + ad[1],
                XY=da[1] - da[0], XZ=ad[1] - ad[0], YZ=dd[0] + dd[1], XYZ=dd[1] - dd[0]))
        return out

    u, l = field(0), field(3)

    def strains(v):
        a, b, c = v
        one = (a["X"], b["Y"], c["Z"], a["Y"] + b["X"], b["Z"] + c["Y"], a["Z"] + c["X"])
        xi = (None, b["XY"], c["XZ"], a["XY"], b["XZ"] + c["XY"], a["XZ"])
        eta = (a["XY"], None, c["YZ"], b["XY"], b["YZ"], a["YZ"] + c["XY"])
        zeta = (a["XZ"], b["YZ"], None, a["YZ"] + b["XZ"], c["YZ"], c["XZ"])
        return one, xi, eta, zeta

    su, sl = strains(u), strains(l)
    total = None
    for kind in range(4):
        eu, el = su[kind], sl[kind]
        normal, tr_u, tr_l = None, None, None
        for k in range(3):
            if eu[k] is not None:
                t = eu[k] * el[k]
                normal = t if normal is None else normal + t
                tr_u = eu[k] if tr_u is None else tr_u + eu[k]
                tr_l = el[k] if tr_l is None else tr_l + el[k]
        gamma = eu[3] * el[3] + eu[4] * el[4] + eu[5] * el[5]
        scale = shear / 16.0 if kind == 0 else shear / 48.0
        part = (2.0 * (normal - tr_u * tr_l * (1.0 / 3.0)) + gamma) * scale
        if kind == 0:
            div_u, div_l = tr_u * 0.25, tr_l * 0.25
        total = part if total is None else total + part
    pure = u[0]["XYZ"] * l[0]["XYZ"] + u[1]["XYZ"] * l[1]["XYZ"] + u[2]["XYZ"] * l[2]["XYZ"]
    total = total + pure * (shear * (10.0 / 3.0) / 144.0)
    return total + div_l * press + mult * div_u - mult * press * (1.0 / bulk)


def kernel(grid, design, flags, disp, adj, press, mult, out,
           vol, vol2, ysum, ybuf, edge, strip, ybuf2, edge2, strip2, pack, pack2,
           nodes, node_rows, rows_in, node_corner, corner_in, modes,
           fl, pr, mu, inv, energy, load_sem, send1, recv1, send2, recv2):
    barrier = pltpu.get_barrier_semaphore()
    count = jnp.int32(0)
    for o in OFFSETS:
        target, ok = peer(grid, o)

        @pl.when(ok)
        def _():
            pl.semaphore_signal(barrier, inc=1, device_id=target, device_id_type=MESH)

        count = count + ok.astype(jnp.int32)

    loads = [
        (design, vol.at[pl.ds(3, 8), pl.ds(0, 8), pl.ds(0, 256)]),
        (disp, nodes.at[pl.ds(0, 3), pl.ds(0, 8)]),
        (adj, nodes.at[pl.ds(3, 3), pl.ds(0, 8)]),
        (flags, fl), (press, pr), (mult, mu),
    ]
    loads = [pltpu.make_async_copy(s, d, load_sem.at[k]) for k, (s, d) in enumerate(loads)]
    for c in loads:
        c.start()
    inverse_weight(grid, inv)
    for c in loads:
        c.wait()
    pack_strips(vol, pack, nodes)
    for f in range(6):
        for i in range(8):
            node_rows[f, i:i + 1, :] = nodes[f, i, 0:1, :]
        node_corner[f:f + 1, :] = nodes[f, 0, 0:1, :]
    node_corner[6:8, :] = jnp.zeros((2, 256), jnp.float32)
    pl.semaphore_wait(barrier, count)

    ex = Exchange(grid, send1, recv1)
    send_volume(ex, vol, ybuf, edge, strip, pack)
    ex.start((-1, 0, 0), nodes.at[:, 0], nodes.at[:, 8])
    ex.start((-1, -1, 0), node_corner, corner_in)
    ex.start((0, -1, 0), node_rows, rows_in)
    for k in range(len(ex.items)):
        ex.finish_recv(k)
    both = assemble(vol, ybuf, edge, strip)
    node_modes(nodes, rows_in, corner_in, both, modes)

    def energies(x, _):
        energy[x] = element_energy(modes, x, pr[x], mu[x])
        return 0

    lax.fori_loop(0, 8, energies, 0)

    denom = math.tanh(sharpness * threshold) + math.tanh(sharpness * (1.0 - threshold))
    base = math.tanh(sharpness * threshold)

    def chain(x, t0, t1):
        for half, t in enumerate((t0, t1)):
            at = pl.ds(128 * half, 128)
            planes = pl.ds(x, 2)
            w = inv[planes, :, at]
            hyper = jnp.tanh(sharpness * (t * w - threshold))
            smooth = (base + hyper) * (1.0 / denom)
            slope = (1.0 - hyper * hyper) * (sharpness / denom)
            value = smooth * smooth * slope * (energy[planes, :, at] * w) * (-3.0 * (1.0 - stiff_floor))
            vol2[pl.ds(x + 3, 2), 0:8, at] = jnp.where(fl[planes, :, at] >= 2, value, 0.0)

    cone_sum(vol, ysum, chain)
    pack_strips(vol2, pack2, None)
    ex2 = Exchange(grid, send2, recv2)
    send_volume(ex2, vol2, ybuf2, edge2, strip2, pack2)
    for k in range(len(ex2.items)):
        ex2.finish_recv(k)
    assemble(vol2, ybuf2, edge2, strip2)

    def final(x, t0, t1):
        planes = pl.ds(x, 2)
        for half, t in enumerate((t0, t1)):
            at = pl.ds(128 * half, 128)
            out[planes, :, at] = jnp.where(fl[planes, :, at] >= 2, t, 0.0)

    cone_sum(vol2, ysum, final)
    for k in range(len(ex.items)):
        ex.finish_send(k)
    for k in range(len(ex2.items)):
        ex2.finish_send(k)


def on_device(grid, *args):
    f32, i32 = jnp.float32, jnp.int32
    V = pltpu.VMEM
    vol = V((14, 16, 384), f32)
    ybuf, edge, strip, pack = V((2, 8, 8, 256), f32), V((2, 2, 3, 8, 256), f32), V((2, 3, 3, 8, 128), f32), V((2, 8, 128), f32)
    brick = V((8, 8, 256), f32)
    dma = pltpu.SemaphoreType.DMA
    return pl.pallas_call(
        functools.partial(kernel, grid),
        out_shape=jax.ShapeDtypeStruct((8, 8, 256), f32),
        in_specs=[pl.BlockSpec(memory_space=pl.ANY)] * 6,
        out_specs=pl.BlockSpec(memory_space=pltpu.VMEM),
        scratch_shapes=[
            vol, vol, V((3, 14, 8, 384), f32), ybuf, edge, strip, ybuf, edge, strip, pack, pack,
            V((6, 9, 8, 256), f32), V((6, 8, 256), f32), V((6, 8, 256), f32), V((8, 256), f32), V((8, 256), f32),
            V((9, 6, 4, 8, 256), f32),
            V((8, 8, 256), i32), brick, brick, brick, brick,
            dma((6,)), dma((29,)), dma((29,)), dma((26,)), dma((26,)),
        ],
        compiler_params=pltpu.CompilerParams(
            collective_id=0, has_side_effects=True, vmem_limit_bytes=32 << 20),
        name="sensitivity",
    )(*args)


def solution(mesh):
    grid = tuple(mesh.shape[a] for a in AXES)
    brick = P("gx", "gy", "gz")
    field = P(None, "gx", "gy", "gz")
    return jax.shard_map(
        functools.partial(on_device, grid), mesh=mesh,
        in_specs=(brick, brick, field, field, brick, brick), out_specs=brick, check_vma=False,
    )
```

time: 138 us -> 40.6 us (0.29)
  the two profiles are of different devices: /device:TPU:249 before, /device:TPU:241 now
where the time goes in v1:
time: 40.6 us; the launch traced here: 40.3 us
  Pallas kernels  34.4 us (85%)
  local copies, waits for them, and re-layouts  5.84 us (14%)
    pallas_call x1, Pallas kernels, on_device(): pl.pallas_call(functools.partial(kernel, grid), out_shape=jax.ShapeDtypeS...  34.4 us
    unnamed x13, local copies, waits for them, and re-layouts  5.84 us

profile of v1, /device:TPU:241, one launch (start us, length us, event | category | flops | bytes accessed | tf_op | source)
XLA Modules:
  0.0 40.3 jit_solution(12842348880342474325)
XLA Ops:
  0.0 0.0 copy-start
  0.0 0.9 %copy-done = f32[3,8,8,256]{3,2,1,0:T(8,128)S(1)} copy-done((f32[3,8,8,256]{3,2,1,0:T(8,128)S(1)}, f32[3,8,8,256]{3,2,1,0:T(8,128)}, u32[]{:S(2)}) %copy-start) | copy-done | bytes 196632
  0.9 0.0 copy-start.1
  0.9 0.9 %copy-done.1 = f32[3,8,8,256]{3,2,1,0:T(8,128)S(1)} copy-done((f32[3,8,8,256]{3,2,1,0:T(8,128)S(1)}, f32[3,8,8,256]{3,2,1,0:T(8,128)}, u32[]{:S(2)}) %copy-start.1) | copy-done | bytes 196632
  1.9 0.0 copy-start.2
  1.9 0.8 %copy-done.2 = f32[8,8,256]{2,1,0:T(8,128)S(1)} copy-done((f32[8,8,256]{2,1,0:T(8,128)S(1)}, f32[8,8,256]{2,1,0:T(8,128)}, u32[]{:S(2)}) %copy-start.2) | copy-done | bytes 65560
  2.7 0.0 copy-start.3
  2.7 0.8 %copy-done.3 = s32[8,8,256]{2,1,0:T(8,128)S(1)} copy-done((s32[8,8,256]{2,1,0:T(8,128)S(1)}, s32[8,8,256]{2,1,0:T(8,128)}, u32[]{:S(2)}) %copy-start.3) | copy-done | bytes 65560
  3.5 0.0 copy-start.4
  3.5 0.8 %copy-done.4 = f32[8,8,256]{2,1,0:T(8,128)S(1)} copy-done((f32[8,8,256]{2,1,0:T(8,128)S(1)}, f32[8,8,256]{2,1,0:T(8,128)}, u32[]{:S(2)}) %copy-start.4) | copy-done | bytes 65560
  4.4 0.0 copy-start.5
  4.4 0.8 %copy-done.5 = f32[8,8,256]{2,1,0:T(8,128)S(1)} copy-done((f32[8,8,256]{2,1,0:T(8,128)S(1)}, f32[8,8,256]{2,1,0:T(8,128)}, u32[]{:S(2)}) %copy-start.5) | copy-done | bytes 65560
  5.2 34.4 %sensitivity.1 = f32[8,8,256]{2,1,0:T(8,128)S(1)} custom-call(f32[8,8,256]{2,1,0:T(8,128)S(1)} %copy-done.2, s32[8,8,256]{2,1,0:T(8,128)S(1)} %copy-done.3, f32[3,8,8,256]{3,2,1,0:T(8,128)S(1)} %copy-done, f32[3,8,8,256]{3,2,1,0:T(8,128)S(1)} %copy-done.1, f32[8,8,256]{2,1,0:T(8,128)S(1)} %copy-done.4, f32[8,8,256]{2,1,0:T(8,128)S(1)} %copy-done.5), custom_call_target="tpu_custom_call" | custom-call | tf_op jit(solution)/shard_map/sensitivity/pallas_call | solution.py:406
  39.7 0.6 %copy.8 = f32[8,8,256]{2,1,0:T(8,128)} copy(f32[8,8,256]{2,1,0:T(8,128)S(1)} %sensitivity.1) | data formatting | bytes 131072
Async XLA Ops:
  0.0 0.9 %copy-start = (f32[3,8,8,256]{3,2,1,0:T(8,128)S(1)}, f32[3,8,8,256]{3,2,1,0:T(8,128)}, u32[]{:S(2)}) copy-start(f32[3,8,8,256]{3,2,1,0:T(8,128)} %disp.1) | copy-start | bytes 589828
  0.9 0.9 %copy-start.1 = (f32[3,8,8,256]{3,2,1,0:T(8,128)S(1)}, f32[3,8,8,256]{3,2,1,0:T(8,128)}, u32[]{:S(2)}) copy-start(f32[3,8,8,256]{3,2,1,0:T(8,128)} %adj.1) | copy-start | bytes 589828
  1.9 0.8 %copy-start.2 = (f32[8,8,256]{2,1,0:T(8,128)S(1)}, f32[8,8,256]{2,1,0:T(8,128)}, u32[]{:S(2)}) copy-start(f32[8,8,256]{2,1,0:T(8,128)} %design.1) | copy-start | bytes 196612
  2.7 0.8 %copy-start.3 = (s32[8,8,256]{2,1,0:T(8,128)S(1)}, s32[8,8,256]{2,1,0:T(8,128)}, u32[]{:S(2)}) copy-start(s32[8,8,256]{2,1,0:T(8,128)} %flags.1) | copy-start | bytes 196612
  3.5 0.8 %copy-start.4 = (f32[8,8,256]{2,1,0:T(8,128)S(1)}, f32[8,8,256]{2,1,0:T(8,128)}, u32[]{:S(2)}) copy-start(f32[8,8,256]{2,1,0:T(8,128)} %press.1) | copy-start | bytes 196612
  4.4 0.8 %copy-start.5 = (f32[8,8,256]{2,1,0:T(8,128)S(1)}, f32[8,8,256]{2,1,0:T(8,128)}, u32[]{:S(2)}) copy-start(f32[8,8,256]{2,1,0:T(8,128)} %mult.1) | copy-start | bytes 196612

commit v2 on v1

v2 whole, which is shorter than its diff:
```python
import functools
import itertools
import math

import jax
import jax.numpy as jnp
from jax import lax
from jax.experimental import pallas as pl
from jax.experimental.pallas import tpu as pltpu
from jax.sharding import PartitionSpec as P

poisson = 0.45
sharpness = 4.0
threshold = 0.5
stiff_floor = 0.001
cone_radius = 3.5

AXES = ("gx", "gy", "gz")
NX, NY, NZ = 8, 8, 256
MESH = pl.DeviceIdType.MESH
NEAR = [(0, 0, 1), (0, 0, -1), (0, 1, 1), (0, -1, 1), (0, 1, -1), (0, -1, -1), (0, 1, 0), (0, -1, 0)]
OFFSETS = [(-1, 0, 0), (1, 0, 0)] + NEAR
COEF = -3.0 * (1.0 - stiff_floor)


def cone_weight(a, b, c):
    r2 = a * a + b * b + c * c
    return cone_radius - math.sqrt(r2) if r2 < cone_radius * cone_radius else 0.0


def place(grid):
    return [lax.axis_index(a) for a in AXES]


def peer(grid, offset):
    at = [lax.axis_index(a) for a in AXES]
    target = tuple(a + o for a, o in zip(at, offset))
    ok = None
    for t, o, n in zip(target, offset, grid):
        if o:
            inside = t >= 0 if o < 0 else t < n
            ok = inside if ok is None else ok & inside
    return target, ok


def opposite(offset):
    return tuple(-o for o in offset)


class Exchange:
    def __init__(self, grid, send, recv):
        self.grid, self.send, self.recv = grid, send, recv
        self.items = []

    def copy(self, index):
        offset, src, dst = self.items[index]
        target, ok = peer(self.grid, offset)
        return ok, pltpu.make_async_remote_copy(
            src_ref=src, dst_ref=dst, send_sem=self.send.at[index], recv_sem=self.recv.at[index],
            device_id=target, device_id_type=MESH,
        )

    def start(self, offset, src, dst):
        self.items.append((offset, src, dst))
        ok, copy = self.copy(len(self.items) - 1)
        pl.when(ok)(copy.start)

    def finish_recv(self, index):
        offset, src, dst = self.items[index]
        _, ok = peer(self.grid, opposite(offset))
        _, copy = self.copy(index)
        pl.when(ok)(copy.wait_recv)

        @pl.when(jnp.logical_not(ok))
        def _():
            dst[...] = jnp.zeros(dst.shape, jnp.float32)

    def finish_send(self, index):
        ok, copy = self.copy(index)
        pl.when(ok)(copy.wait_send)


def roll(value, by, axis):
    by = by % value.shape[axis]
    return value if by == 0 else pltpu.roll(value, by, axis)


def iota(shape, dim):
    return lax.broadcasted_iota(jnp.int32, shape, dim)


def cone_sum(vol, ysum, emit):
    row = iota((2, 8, 384), 1)

    def rows(p, _):
        at = pl.ds(2 * p, 2)
        low, high = vol[at, 0:8, :], vol[at, 8:16, :]
        for b in (1, 2, 3):
            up = roll(jnp.where(row < b, high, low), -b, 1)
            down = roll(jnp.where(row >= 8 - b, high, low), b, 1)
            ysum[b - 1, at] = up + down
        return 0

    lax.fori_loop(0, 7, rows, 0)
    lane = iota((2, 8, 128), 2)

    def planes(p, _):
        x = 2 * p
        sums = {}

        def get(b, k):
            return vol[pl.ds(x + k, 2), 0:8, :] if b == 0 else ysum[b - 1, pl.ds(x + k, 2)]

        for a in range(4):
            for b in range(4):
                if a * a + b * b < 12.25:
                    sums[a, b] = get(b, 3) if a == 0 else get(b, 3 - a) + get(b, 3 + a)
        groups = {}
        for (a, b), value in sums.items():
            key = (min(a, b), max(a, b))
            groups[key] = groups[key] + value if key in groups else value
        total = None
        for c in range(4):
            g = None
            for (a, b), value in groups.items():
                w = cone_weight(a, b, c)
                if w > 0:
                    g = value * w if g is None else g + value * w
            g0, g1, gh = g[:, :, 0:128], g[:, :, 128:256], g[:, :, 256:384]
            if c == 0:
                t0, t1 = g0, g1
            else:
                t0 = t0 + roll(jnp.where(lane < c, g1, g0), -c, 2) + roll(
                    jnp.where(lane >= 128 - c, gh, g0), c, 2)
                t1 = t1 + roll(jnp.where(lane < c, gh, g1), -c, 2) + roll(
                    jnp.where(lane >= 128 - c, g0, g1), c, 2)
        emit(x, t0, t1)
        return 0

    lax.fori_loop(0, 4, planes, 0)


def inverse_weight(grid, out):
    gx, gy, gz = [lax.axis_index(a) for a in AXES]
    y = gy * NY + iota((NY, NZ), 0)
    z = gz * NZ + iota((NY, NZ), 1)

    def pairs(pos, by, size):
        def inside(v):
            return ((v >= 0) & (v < size)).astype(jnp.float32)
        return inside(pos + by) + inside(pos - by) if by else inside(pos)

    ys = [None] + [pairs(y, b, grid[1] * NY) for b in (1, 2, 3)]
    zs = [None] + [pairs(z, c, grid[2] * NZ) for c in (1, 2, 3)]
    fs = []
    for a in range(4):
        f = jnp.full((NY, NZ), 0.0, jnp.float32)
        for b in range(4):
            for c in range(4):
                w = cone_weight(a, b, c)
                if w > 0:
                    term = jnp.float32(w)
                    term = term if b == 0 else term * ys[b]
                    term = term if c == 0 else term * zs[c]
                    f = f + term
        fs.append(f)
    for k in range(14):
        px = gx * NX + k - 3
        w = fs[0] * pairs(px, 0, grid[0] * NX)
        for a in (1, 2, 3):
            w = w + fs[a] * pairs(px, a, grid[0] * NX)
        out[k] = 1.0 / w


def pack_rows(vol, first, half, rows):
    row = iota((8, 256), 0)
    for k in range(half):
        a, b = vol[first + k, 0:8, 0:256], vol[first + half + k, 0:8, 0:256]
        b = roll(b, 4, 0)
        rows[0, k] = jnp.where(row < 4, a, b)
        rows[1, k] = jnp.where(row < 4, b, a)


def pack_strips(vol, planes, slot, pack, nodes):
    lane = iota((8, 128), 1)
    down, up = None, None
    for i in range(planes):
        first, last = vol[i, 0:8, 0:128], vol[i, 0:8, 128:256]
        d, u = roll(first, slot * i, 1), roll(last, slot * i, 1)
        if i == 0:
            down, up = d, u
        else:
            down = jnp.where((lane >= slot * i) & (lane < slot * i + 3), d, down)
            up = jnp.where((lane >= slot * i - 3) & (lane < slot * i), u, up)
        if nodes is not None:
            for f in range(6):
                n = roll(nodes[f, 1 + i, :, 0:128], slot * i + 3 + f, 1)
                down = jnp.where(lane == slot * i + 3 + f, n, down)
    pack[0] = down
    pack[1] = up


def send_near(ex, rows, pack, rows_in, strip):
    for o in NEAR:
        _, dy, dz = o
        if dz:
            k = 0 if dz < 0 else 1
            ex.start(o, pack.at[k], strip.at[k, 1 - dy])
        else:
            k = 0 if dy < 0 else 1
            ex.start(o, rows.at[k], rows_in.at[k])


def assemble(vol, half, slot, rows_in, strip):
    row = iota((8, 256), 0)
    rowl = iota((8, 128), 0)
    lane = iota((8, 128), 1)
    for k in range(half):
        from_upper, from_lower = rows_in[0, k], rows_in[1, k]
        vol[k, 8:16, 0:256] = jnp.where(row < 4, from_upper, from_lower)
        vol[half + k, 8:16, 0:256] = roll(jnp.where(row < 4, from_lower, from_upper), 4, 0)
    both = [jnp.where((lane & (slot - 1)) < slot - 4, strip[0, dy], strip[1, dy]) for dy in range(3)]
    side = jnp.where(rowl < 4, both[2], both[0])
    for k in range(2 * half):
        vol[k, 0:8, 256:384] = roll(both[1], -slot * k, 1)
        vol[k, 8:16, 256:384] = roll(side, -slot * k, 1)
    return both[1], both[2]


def plane_sums(vol, fs, psum):
    row = iota((8, 384), 0)
    lane = iota((8, 128), 1)

    def shifts(t, c):
        t0, t1, th = t[:, 0:128], t[:, 128:256], t[:, 256:384]
        u0 = roll(jnp.where(lane < c, t1, t0), -c, 1) + roll(jnp.where(lane >= 128 - c, th, t0), c, 1)
        u1 = roll(jnp.where(lane < c, th, t1), -c, 1) + roll(jnp.where(lane >= 128 - c, t0, t1), c, 1)
        return u0, u1

    def plane(p, _):
        low, high = vol[p, 0:8, :], vol[p, 8:16, :]
        ys = [low]
        for b in (1, 2, 3):
            up = roll(jnp.where(row < b, high, low), -b, 0)
            down = roll(jnp.where(row >= 8 - b, high, low), b, 0)
            ys.append(up + down)
        groups = {}
        for b in range(4):
            for c in range(4):
                if b * b + c * c < 12.25:
                    v = (ys[b][:, 0:128], ys[b][:, 128:256]) if c == 0 else shifts(ys[b], c)
                    key = (min(b, c), max(b, c))
                    groups[key] = tuple(s + t for s, t in zip(groups[key], v)) if key in groups else v
        for a in range(4):
            for half in range(2):
                f = None
                for (b, c), v in groups.items():
                    w = cone_weight(a, b, c)
                    if w > 0:
                        f = v[half] * w if f is None else f + v[half] * w
                fs[a, p, :, pl.ds(128 * half, 128)] = f
        return 0

    lax.fori_loop(0, 8, plane, 0)
    for k in range(14):
        total = None
        for a in range(-3, 4):
            p = k - 3 + a
            if 0 <= p < 8:
                total = fs[abs(a), p] if total is None else total + fs[abs(a), p]
        psum[k] = total


def node_halo(halo, main, side):
    lane = iota((8, 128), 1)
    for p in range(8):
        a = roll(main, -(16 * p + 3), 1)
        b = roll(roll(side, -(16 * p + 3) + 8, 1), -1, 0)
        halo[1 + p, :, 256:384] = jnp.where(lane < 8, a, b)


def node_modes(nodes, halo, modes, q):
    lane = iota((8, 128), 1)
    row = iota((8, 128), 0)
    hs = halo[q, :, 256:384]
    hm = jnp.where(row == 7, roll(hs, -8, 1), roll(hs, -1, 0))
    for f in range(6):
        n = [nodes[f, q, :, 0:128], nodes[f, q, :, 128:256]]
        e = [halo[q, f:f + 1, 0:128], halo[q, f:f + 1, 128:256]]
        m = [jnp.where(row == 7, jnp.broadcast_to(e[k], (8, 128)), roll(n[k], -1, 0)) for k in range(2)]

        def up(v, h):
            v0, v1 = roll(v[0], -1, 1), roll(v[1], -1, 1)
            return jnp.where(lane == 127, v1, v0), jnp.where(lane == 127, roll(h, 127 - f, 1), v1)

        s, r = up(n, hs), up(m, hm)
        for k in range(2):
            a, d = n[k] + s[k], s[k] - n[k]
            ay, dy = m[k] + r[k], r[k] - m[k]
            at = pl.ds(128 * k, 128)
            modes[q, f, 0, :, at] = a + ay
            modes[q, f, 1, :, at] = d + dy
            modes[q, f, 2, :, at] = ay - a
            modes[q, f, 3, :, at] = dy - d


def element_energy(modes, x, press, mult):
    shear = 1.0 / (2.0 * (1.0 + poisson))
    bulk = 1.0 / (3.0 * (1.0 - 2.0 * poisson))

    def both_of(f, m):
        return modes[x, f, m], modes[x + 1, f, m]

    def field(base):
        out = []
        for c in range(3):
            aa, ad, da, dd = (both_of(base + c, m) for m in range(4))
            out.append(dict(
                X=aa[1] - aa[0], Y=da[0] + da[1], Z=ad[0] + ad[1],
                XY=da[1] - da[0], XZ=ad[1] - ad[0], YZ=dd[0] + dd[1], XYZ=dd[1] - dd[0]))
        return out

    u, l = field(0), field(3)

    def strains(v):
        a, b, c = v
        one = (a["X"], b["Y"], c["Z"], a["Y"] + b["X"], b["Z"] + c["Y"], a["Z"] + c["X"])
        xi = (None, b["XY"], c["XZ"], a["XY"], b["XZ"] + c["XY"], a["XZ"])
        eta = (a["XY"], None, c["YZ"], b["XY"], b["YZ"], a["YZ"] + c["XY"])
        zeta = (a["XZ"], b["YZ"], None, a["YZ"] + b["XZ"], c["YZ"], c["XZ"])
        return one, xi, eta, zeta

    su, sl = strains(u), strains(l)
    total = None
    for kind in range(4):
        eu, el = su[kind], sl[kind]
        normal, tr_u, tr_l = None, None, None
        for k in range(3):
            if eu[k] is not None:
                t = eu[k] * el[k]
                normal = t if normal is None else normal + t
                tr_u = eu[k] if tr_u is None else tr_u + eu[k]
                tr_l = el[k] if tr_l is None else tr_l + el[k]
        gamma = eu[3] * el[3] + eu[4] * el[4] + eu[5] * el[5]
        scale = shear / 16.0 if kind == 0 else shear / 48.0
        part = (2.0 * (normal - tr_u * tr_l * (1.0 / 3.0)) + gamma) * scale
        if kind == 0:
            div_u, div_l = tr_u * 0.25, tr_l * 0.25
        total = part if total is None else total + part
    pure = u[0]["XYZ"] * l[0]["XYZ"] + u[1]["XYZ"] * l[1]["XYZ"] + u[2]["XYZ"] * l[2]["XYZ"]
    total = total + pure * (shear * (10.0 / 3.0) / 144.0)
    return total + div_l * press + mult * div_u - mult * press * (1.0 / bulk)


def kernel(grid, design, flags, disp, adj, press, mult, out,
           vol, vol2, fs, ysum, psum, sums_in, rows, rows_in, strip, pack, rows2, rows_in2, strip2, pack2,
           nodes, node_rows, halo, modes, aux, fl, inv, energy,
           load_sem, send1, recv1, send2, recv2, send3, recv3):
    barrier = pltpu.get_barrier_semaphore()
    count = jnp.int32(0)
    for o in OFFSETS:
        target, ok = peer(grid, o)

        @pl.when(ok)
        def _():
            pl.semaphore_signal(barrier, inc=1, device_id=target, device_id_type=MESH)

        count = count + ok.astype(jnp.int32)

    own = pl.ds(1, 8)
    loads = [
        (design, vol.at[:, pl.ds(0, 8), pl.ds(0, 256)]),
        (disp, nodes.at[pl.ds(0, 3), own]),
        (adj, nodes.at[pl.ds(3, 3), own]),
        (flags, fl), (press, aux.at[own, 0]), (mult, aux.at[own, 1]),
    ]
    loads = [pltpu.make_async_copy(s, d, load_sem.at[k]) for k, (s, d) in enumerate(loads)]
    for c in loads:
        c.start()
    inverse_weight(grid, inv)
    for c in loads:
        c.wait()
    for x in range(8):
        aux[1 + x, 2] = jnp.where(fl[x] >= 2, inv[3 + x] * COEF, 0.0)
    pack_strips(vol, 8, 16, pack, nodes)
    pack_rows(vol, 0, 4, rows)
    for p in range(8):
        for f in range(6):
            node_rows[p, f:f + 1, :] = nodes[f, 1 + p, 0:1, :]
        node_rows[p, 6:8, :] = jnp.zeros((2, 256), jnp.float32)
    pl.semaphore_wait(barrier, count)

    lower, upper = (-1, 0, 0), (1, 0, 0)
    far = Exchange(grid, send2, recv2)
    far.start(lower, nodes.at[:, 1], nodes.at[:, 9])
    far.start(upper, nodes.at[:, 8], nodes.at[:, 0])
    far.start(upper, aux.at[8], aux.at[0])
    near = Exchange(grid, send1, recv1)
    send_near(near, rows, pack, rows_in, strip)
    near.start((0, -1, 0), node_rows, halo.at[own, :, pl.ds(0, 256)])
    for k in range(9):
        near.finish_recv(k)

    main, side = assemble(vol, 4, 16, rows_in, strip)
    plane_sums(vol, fs, psum)
    far.start(lower, psum.at[pl.ds(0, 6)], sums_in.at[1])
    far.start(upper, psum.at[pl.ds(8, 6)], sums_in.at[0])
    node_halo(halo, main, side)
    far.start(lower, halo.at[1], halo.at[9])
    far.start(upper, halo.at[8], halo.at[0])

    def own_modes(q, _):
        node_modes(nodes, halo, modes, q)
        return 0

    lax.fori_loop(1, 9, own_modes, 0)

    def scaled(x):
        return element_energy(modes, x + 1, aux[x + 1, 0], aux[x + 1, 1]) * aux[x + 1, 2]

    def energies(x, _):
        energy[x + 3] = scaled(x)
        return 0

    lax.fori_loop(0, 7, energies, 0)
    far.start(lower, energy.at[pl.ds(3, 3)], energy.at[pl.ds(11, 3)])
    far.start(upper, energy.at[pl.ds(8, 2)], energy.at[pl.ds(0, 2)])
    for k in (0, 1, 2, 5, 6):
        far.finish_recv(k)
    for q in (0, 9):
        node_modes(nodes, halo, modes, q)
    for x in (-1, 7):
        energy[x + 3] = scaled(x)
    for k in (3, 4, 7, 8):
        far.finish_recv(k)

    denom = math.tanh(sharpness * threshold) + math.tanh(sharpness * (1.0 - threshold))
    base = math.tanh(sharpness * threshold)
    for k in range(14):
        total = psum[k]
        if k < 6:
            total = total + sums_in[0, k]
        if k >= 8:
            total = total + sums_in[1, k - 8]
        hyper = jnp.tanh(sharpness * (total * inv[k] - threshold))
        smooth = (base + hyper) * (1.0 / denom)
        slope = (1.0 - hyper * hyper) * (sharpness / denom)
        vol2[k, 0:8, 0:256] = smooth * smooth * slope * energy[k]

    pack_strips(vol2, 14, 8, pack2, None)
    pack_rows(vol2, 0, 7, rows2)
    last = Exchange(grid, send3, recv3)
    send_near(last, rows2, pack2, rows_in2, strip2)
    for k in range(8):
        last.finish_recv(k)
    assemble(vol2, 7, 8, rows_in2, strip2)

    def final(x, t0, t1):
        planes = pl.ds(x, 2)
        for half, t in enumerate((t0, t1)):
            at = pl.ds(128 * half, 128)
            out[planes, :, at] = jnp.where(fl[planes, :, at] >= 2, t, 0.0)

    cone_sum(vol2, ysum, final)
    for ex in (near, far, last):
        for k in range(len(ex.items)):
            ex.finish_send(k)


def on_device(grid, *args):
    f32, i32 = jnp.float32, jnp.int32
    V = pltpu.VMEM
    dma = pltpu.SemaphoreType.DMA
    strip, pack = V((2, 3, 8, 128), f32), V((2, 8, 128), f32)
    return pl.pallas_call(
        functools.partial(kernel, grid),
        out_shape=jax.ShapeDtypeStruct((8, 8, 256), f32),
        in_specs=[pl.BlockSpec(memory_space=pl.ANY)] * 6,
        out_specs=pl.BlockSpec(memory_space=pltpu.VMEM),
        scratch_shapes=[
            V((8, 16, 384), f32), V((14, 16, 384), f32), V((4, 8, 8, 256), f32), V((3, 14, 8, 384), f32),
            V((14, 8, 256), f32), V((2, 6, 8, 256), f32),
            V((2, 4, 8, 256), f32), V((2, 4, 8, 256), f32), strip, pack,
            V((2, 7, 8, 256), f32), V((2, 7, 8, 256), f32), strip, pack,
            V((6, 10, 8, 256), f32), V((8, 8, 256), f32), V((10, 8, 384), f32), V((10, 6, 4, 8, 256), f32),
            V((9, 3, 8, 256), f32), V((8, 8, 256), i32), V((14, 8, 256), f32), V((14, 8, 256), f32),
            dma((6,)), dma((9,)), dma((9,)), dma((9,)), dma((9,)), dma((8,)), dma((8,)),
        ],
        compiler_params=pltpu.CompilerParams(
            collective_id=0, has_side_effects=True, vmem_limit_bytes=63 << 20),
        name="sensitivity",
    )(*args)


def solution(mesh):
    grid = tuple(mesh.shape[a] for a in AXES)
    brick = P("gx", "gy", "gz")
    field = P(None, "gx", "gy", "gz")
    return jax.shard_map(
        functools.partial(on_device, grid), mesh=mesh,
        in_specs=(brick, brick, field, field, brick, brick), out_specs=brick, check_vma=False,
    )
```

time: 40.6 us -> 29.9 us (0.74)
  the two profiles are of different devices: /device:TPU:241 before, /device:TPU:135 now
where the time goes in v2:
time: 29.9 us; the launch traced here: 29.7 us
  Pallas kernels  28.2 us (94%)
  local copies, waits for them, and re-layouts  1.47 us (5%)
    pallas_call x1, Pallas kernels, on_device(): pl.pallas_call(functools.partial(kernel, grid), out_shape=jax.ShapeDtypeS...  28.2 us
    unnamed x1, local copies, waits for them, and re-layouts  1.47 us

profile of v2, /device:TPU:135, one launch (start us, length us, event | category | flops | bytes accessed | tf_op | source)
XLA Modules:
  0.0 29.7 jit_solution(1781176087032388923)
XLA Ops:
  0.0 28.2 %sensitivity.1 = f32[8,8,256]{2,1,0:T(8,128)} custom-call(f32[8,8,256]{2,1,0:T(8,128)} %design.1, s32[8,8,256]{2,1,0:T(8,128)} %flags.1, f32[3,8,8,256]{3,2,1,0:T(8,128)} %disp.1, f32[3,8,8,256]{3,2,1,0:T(8,128)} %adj.1, f32[8,8,256]{2,1,0:T(8,128)} %press.1, f32[8,8,256]{2,1,0:T(8,128)} %mult.1), custom_call_target="tpu_custom_call" | custom-call | tf_op jit(solution)/shard_map/sensitivity/pallas_call | solution.py:475
  28.2 1.5 %copy.8 = f32[8,8,256]{2,1,0:T(8,128)} copy(f32[8,8,256]{2,1,0:T(8,128)} %sensitivity.1) | data formatting | bytes 131072

commit v3 on v2

--- a/solution.py
+++ b/solution.py
@@ -19,7 +19,6 @@
 NX, NY, NZ = 8, 8, 256
 MESH = pl.DeviceIdType.MESH
 NEAR = [(0, 0, 1), (0, 0, -1), (0, 1, 1), (0, -1, 1), (0, 1, -1), (0, -1, -1), (0, 1, 0), (0, -1, 0)]
-OFFSETS = [(-1, 0, 0), (1, 0, 0)] + NEAR
 COEF = -3.0 * (1.0 - stiff_floor)
 
 
@@ -355,17 +354,29 @@
 def kernel(grid, design, flags, disp, adj, press, mult, out,
            vol, vol2, fs, ysum, psum, sums_in, rows, rows_in, strip, pack, rows2, rows_in2, strip2, pack2,
            nodes, node_rows, halo, modes, aux, fl, inv, energy,
-           load_sem, send1, recv1, send2, recv2, send3, recv3):
+           load_sem, ready, send1, recv1, send2, recv2, send3, recv3):
     barrier = pltpu.get_barrier_semaphore()
+    at = [lax.axis_index(a) for a in AXES]
+    first, last_x, half = 0, grid[0] - 1, grid[0] // 2
+    beside = (at[0] == half - 1) | (at[0] == half)
     count = jnp.int32(0)
-    for o in OFFSETS:
-        target, ok = peer(grid, o)
-
+
+    def greet(target, ok, counts):
         @pl.when(ok)
         def _():
             pl.semaphore_signal(barrier, inc=1, device_id=target, device_id_type=MESH)
 
-        count = count + ok.astype(jnp.int32)
+        return count + jnp.int32(1) * counts
+
+    for o in NEAR:
+        target, ok = peer(grid, o)
+        count = greet(target, ok, ok)
+    for dx in (-1, 1):
+        target, ok = peer(grid, (dx, 0, 0))
+        ok = ok & (at[0] != (half if dx < 0 else half - 1))
+        count = greet(target, ok, ok)
+    for end in (first, last_x):
+        count = greet((end, at[1], at[2]), beside, 2 * (at[0] == end))
 
     own = pl.ds(1, 8)
     loads = [
@@ -389,18 +400,26 @@
             node_rows[p, f:f + 1, :] = nodes[f, 1 + p, 0:1, :]
         node_rows[p, 6:8, :] = jnp.zeros((2, 256), jnp.float32)
     pl.semaphore_wait(barrier, count)
+    for end, to in ((first, half - 1), (last_x, half)):
+        @pl.when(at[0] == end)
+        def _():
+            pl.semaphore_signal(ready, inc=1, device_id=(to, at[1], at[2]), device_id_type=MESH)
+
+    near = Exchange(grid, send1, recv1)
+    send_near(near, rows, pack, rows_in, strip)
+    near.start((0, -1, 0), node_rows, halo.at[own, :, pl.ds(0, 256)])
+    for k in range(9):
+        near.finish_recv(k)
+
+    @pl.when(beside)
+    def _():
+        pl.semaphore_wait(ready, 1)
 
     lower, upper = (-1, 0, 0), (1, 0, 0)
     far = Exchange(grid, send2, recv2)
     far.start(lower, nodes.at[:, 1], nodes.at[:, 9])
     far.start(upper, nodes.at[:, 8], nodes.at[:, 0])
     far.start(upper, aux.at[8], aux.at[0])
-    near = Exchange(grid, send1, recv1)
-    send_near(near, rows, pack, rows_in, strip)
-    near.start((0, -1, 0), node_rows, halo.at[own, :, pl.ds(0, 256)])
-    for k in range(9):
-        near.finish_recv(k)
-
     main, side = assemble(vol, 4, 16, rows_in, strip)
     plane_sums(vol, fs, psum)
     far.start(lower, psum.at[pl.ds(0, 6)], sums_in.at[1])
@@ -484,7 +503,7 @@
             V((2, 7, 8, 256), f32), V((2, 7, 8, 256), f32), strip, pack,
             V((6, 10, 8, 256), f32), V((8, 8, 256), f32), V((10, 8, 384), f32), V((10, 6, 4, 8, 256), f32),
             V((9, 3, 8, 256), f32), V((8, 8, 256), i32), V((14, 8, 256), f32), V((14, 8, 256), f32),
-            dma((6,)), dma((9,)), dma((9,)), dma((9,)), dma((9,)), dma((8,)), dma((8,)),
+            dma((6,)), pltpu.SemaphoreType.REGULAR, dma((9,)), dma((9,)), dma((9,)), dma((9,)), dma((8,)), dma((8,)),
         ],
         compiler_params=pltpu.CompilerParams(
             collective_id=0, has_side_effects=True, vmem_limit_bytes=63 << 20),

time: 29.9 us -> 28.1 us (0.940)
  the two profiles are of different devices: /device:TPU:135 before, /device:TPU:199 now
where the time goes in v3:
time: 28.1 us; the launch traced here: 27.9 us
  Pallas kernels  26.4 us (94%)
  local copies, waits for them, and re-layouts  1.47 us (5%)
    pallas_call x1, Pallas kernels, on_device(): pl.pallas_call(functools.partial(kernel, grid), out_shape=jax.ShapeDtypeS...  26.4 us
    unnamed x1, local copies, waits for them, and re-layouts  1.47 us

profile of v3, /device:TPU:199, one launch (start us, length us, event | category | flops | bytes accessed | tf_op | source)
XLA Modules:
  0.0 27.9 jit_solution(2239904476649877708)
XLA Ops:
  0.0 26.4 %sensitivity.1 = f32[8,8,256]{2,1,0:T(8,128)} custom-call(f32[8,8,256]{2,1,0:T(8,128)} %design.1, s32[8,8,256]{2,1,0:T(8,128)} %flags.1, f32[3,8,8,256]{3,2,1,0:T(8,128)} %disp.1, f32[3,8,8,256]{3,2,1,0:T(8,128)} %adj.1, f32[8,8,256]{2,1,0:T(8,128)} %press.1, f32[8,8,256]{2,1,0:T(8,128)} %mult.1), custom_call_target="tpu_custom_call" | custom-call | tf_op jit(solution)/shard_map/sensitivity/pallas_call | solution.py:494
  26.4 1.5 %copy.8 = f32[8,8,256]{2,1,0:T(8,128)} copy(f32[8,8,256]{2,1,0:T(8,128)} %sensitivity.1) | data formatting | bytes 131072

commit v4 on v3

--- a/solution.py
+++ b/solution.py
@@ -18,7 +18,7 @@
 AXES = ("gx", "gy", "gz")
 NX, NY, NZ = 8, 8, 256
 MESH = pl.DeviceIdType.MESH
-NEAR = [(0, 0, 1), (0, 0, -1), (0, 1, 1), (0, -1, 1), (0, 1, -1), (0, -1, -1), (0, 1, 0), (0, -1, 0)]
+NEAR = [(0, 1, 1), (0, -1, 1), (0, 1, -1), (0, -1, -1), (0, -1, 0), (0, 1, 0), (0, 0, 1), (0, 0, -1)]
 COEF = -3.0 * (1.0 - stiff_floor)
 
 
@@ -59,10 +59,16 @@
             device_id=target, device_id_type=MESH,
         )
 
+    def add(self, offset, src, dst):
+        self.items.append((offset, src, dst))
+        return len(self.items) - 1
+
+    def begin(self, index, when=None):
+        ok, copy = self.copy(index)
+        pl.when(ok if when is None else ok & when)(copy.start)
+
     def start(self, offset, src, dst):
-        self.items.append((offset, src, dst))
-        ok, copy = self.copy(len(self.items) - 1)
-        pl.when(ok)(copy.start)
+        self.begin(self.add(offset, src, dst))
 
     def finish_recv(self, index):
         offset, src, dst = self.items[index]
@@ -368,16 +374,8 @@
 
         return count + jnp.int32(1) * counts
 
-    for o in NEAR:
-        target, ok = peer(grid, o)
-        count = greet(target, ok, ok)
-    for dx in (-1, 1):
-        target, ok = peer(grid, (dx, 0, 0))
-        ok = ok & (at[0] != (half if dx < 0 else half - 1))
-        count = greet(target, ok, ok)
     for end in (first, last_x):
         count = greet((end, at[1], at[2]), beside, 2 * (at[0] == end))
-
     own = pl.ds(1, 8)
     loads = [
         (design, vol.at[:, pl.ds(0, 8), pl.ds(0, 256)]),
@@ -388,11 +386,15 @@
     loads = [pltpu.make_async_copy(s, d, load_sem.at[k]) for k, (s, d) in enumerate(loads)]
     for c in loads:
         c.start()
-    inverse_weight(grid, inv)
-    for c in loads:
+    for o in NEAR:
+        target, ok = peer(grid, o)
+        count = greet(target, ok, ok)
+    for dx in (-1, 1):
+        target, ok = peer(grid, (dx, 0, 0))
+        ok = ok & (at[0] != (half if dx < 0 else half - 1))
+        count = greet(target, ok, ok)
+    for c in loads[:3]:
         c.wait()
-    for x in range(8):
-        aux[1 + x, 2] = jnp.where(fl[x] >= 2, inv[3 + x] * COEF, 0.0)
     pack_strips(vol, 8, 16, pack, nodes)
     pack_rows(vol, 0, 4, rows)
     for p in range(8):
@@ -408,8 +410,11 @@
     near = Exchange(grid, send1, recv1)
     send_near(near, rows, pack, rows_in, strip)
     near.start((0, -1, 0), node_rows, halo.at[own, :, pl.ds(0, 256)])
-    for k in range(9):
-        near.finish_recv(k)
+    inverse_weight(grid, inv)
+    for c in loads[3:]:
+        c.wait()
+    for x in range(8):
+        aux[1 + x, 2] = jnp.where(fl[x] >= 2, inv[3 + x] * COEF, 0.0)
 
     @pl.when(beside)
     def _():
@@ -420,37 +425,47 @@
     far.start(lower, nodes.at[:, 1], nodes.at[:, 9])
     far.start(upper, nodes.at[:, 8], nodes.at[:, 0])
     far.start(upper, aux.at[8], aux.at[0])
+    for k in range(9):
+        near.finish_recv(k)
     main, side = assemble(vol, 4, 16, rows_in, strip)
+    node_halo(halo, main, side)
+    far.start(lower, halo.at[1], halo.at[9])
+    far.start(upper, halo.at[8], halo.at[0])
     plane_sums(vol, fs, psum)
     far.start(lower, psum.at[pl.ds(0, 6)], sums_in.at[1])
     far.start(upper, psum.at[pl.ds(8, 6)], sums_in.at[0])
-    node_halo(halo, main, side)
-    far.start(lower, halo.at[1], halo.at[9])
-    far.start(upper, halo.at[8], halo.at[0])
-
-    def own_modes(q, _):
-        node_modes(nodes, halo, modes, q)
-        return 0
-
-    lax.fori_loop(1, 9, own_modes, 0)
 
     def scaled(x):
         return element_energy(modes, x + 1, aux[x + 1, 0], aux[x + 1, 1]) * aux[x + 1, 2]
 
-    def energies(x, _):
+    down_first = (at[0] == half).astype(jnp.int32)
+
+    def own_modes(i, _):
+        node_modes(nodes, halo, modes, jnp.where(down_first == 1, 1 + i, 8 - i))
+        return 0
+
+    def energies(i, _):
+        x = jnp.where(down_first == 1, i, 6 - i)
         energy[x + 3] = scaled(x)
         return 0
 
-    lax.fori_loop(0, 7, energies, 0)
-    far.start(lower, energy.at[pl.ds(3, 3)], energy.at[pl.ds(11, 3)])
-    far.start(upper, energy.at[pl.ds(8, 2)], energy.at[pl.ds(0, 2)])
-    for k in (0, 1, 2, 5, 6):
+    lax.fori_loop(0, 4, own_modes, 0)
+    lax.fori_loop(0, 3, energies, 0)
+    far.add(lower, energy.at[pl.ds(3, 3)], energy.at[pl.ds(11, 3)])
+    far.add(upper, energy.at[pl.ds(8, 2)], energy.at[pl.ds(0, 2)])
+    far.begin(7, down_first == 1)
+    far.begin(8, down_first == 0)
+    lax.fori_loop(4, 8, own_modes, 0)
+    lax.fori_loop(3, 7, energies, 0)
+    far.begin(7, down_first == 0)
+    far.begin(8, down_first == 1)
+    for k in (0, 1, 2, 3, 4):
         far.finish_recv(k)
     for q in (0, 9):
         node_modes(nodes, halo, modes, q)
     for x in (-1, 7):
         energy[x + 3] = scaled(x)
-    for k in (3, 4, 7, 8):
+    for k in (5, 6, 7, 8):
         far.finish_recv(k)
 
     denom = math.tanh(sharpness * threshold) + math.tanh(sharpness * (1.0 - threshold))
@@ -493,7 +508,7 @@
     strip, pack = V((2, 3, 8, 128), f32), V((2, 8, 128), f32)
     return pl.pallas_call(
         functools.partial(kernel, grid),
-        out_shape=jax.ShapeDtypeStruct((8, 8, 256), f32),
+        out_shape=pltpu.VMEM((8, 8, 256), f32),
         in_specs=[pl.BlockSpec(memory_space=pl.ANY)] * 6,
         out_specs=pl.BlockSpec(memory_space=pltpu.VMEM),
         scratch_shapes=[

time: 28.1 us -> 25.5 us (0.907)
  Pallas kernels: 26.4 us -> 24.8 us
  local copies, waits for them, and re-layouts: 1.47 us -> 0.63 us
    pallas_call x1, Pallas kernels: 26.4 us -> 24.8 us  [on_device(): pl.pallas_call(functools.partial(kernel, grid), out_shape=pltpu.VMEM((8,...]
    unnamed x1, local copies, waits for them, and re-layouts: 1.47 us -> 0.63 us
where the time goes in v4:
time: 25.5 us; the launch traced here: 25.4 us
  Pallas kernels  24.8 us (97%)
  local copies, waits for them, and re-layouts  0.63 us (2%)
    pallas_call x1, Pallas kernels, on_device(): pl.pallas_call(functools.partial(kernel, grid), out_shape=pltpu.VMEM((8,...  24.8 us
    unnamed x1, local copies, waits for them, and re-layouts  0.63 us

profile of v4, /device:TPU:199, one launch (start us, length us, event | category | flops | bytes accessed | tf_op | source)
XLA Modules:
  0.0 25.4 jit_solution(14500906417387947499)
XLA Ops:
  0.0 24.8 %sensitivity.1 = f32[8,8,256]{2,1,0:T(8,128)S(1)} custom-call(f32[8,8,256]{2,1,0:T(8,128)} %design.1, s32[8,8,256]{2,1,0:T(8,128)} %flags.1, f32[3,8,8,256]{3,2,1,0:T(8,128)} %disp.1, f32[3,8,8,256]{3,2,1,0:T(8,128)} %adj.1, f32[8,8,256]{2,1,0:T(8,128)} %press.1, f32[8,8,256]{2,1,0:T(8,128)} %mult.1), custom_call_target="tpu_custom_call" | custom-call | tf_op jit(solution)/shard_map/sensitivity/pallas_call | solution.py:509
  24.8 0.6 %copy.8 = f32[8,8,256]{2,1,0:T(8,128)} copy(f32[8,8,256]{2,1,0:T(8,128)S(1)} %sensitivity.1) | data formatting | bytes 131072

commit v5 on v4

v5 whole, which is shorter than its diff:
```python
import functools
import itertools
import math

import jax
import jax.numpy as jnp
from jax import lax
from jax.experimental import pallas as pl
from jax.experimental.pallas import tpu as pltpu
from jax.sharding import PartitionSpec as P

poisson = 0.45
sharpness = 4.0
threshold = 0.5
stiff_floor = 0.001
cone_radius = 3.5

AXES = ("gx", "gy", "gz")
NX, NY, NZ = 8, 8, 256
MESH = pl.DeviceIdType.MESH
NEAR = [(0, 1, 1), (0, -1, 1), (0, 1, -1), (0, -1, -1), (0, -1, 0), (0, 1, 0), (0, 0, 1), (0, 0, -1)]
COEF = -3.0 * (1.0 - stiff_floor)


def cone_weight(a, b, c):
    r2 = a * a + b * b + c * c
    return cone_radius - math.sqrt(r2) if r2 < cone_radius * cone_radius else 0.0


def place(grid):
    return [lax.axis_index(a) for a in AXES]


def peer(grid, offset):
    at = [lax.axis_index(a) for a in AXES]
    target = tuple(a + o for a, o in zip(at, offset))
    ok = None
    for t, o, n in zip(target, offset, grid):
        if o:
            inside = t >= 0 if o < 0 else t < n
            ok = inside if ok is None else ok & inside
    return target, ok


def opposite(offset):
    return tuple(-o for o in offset)


class Exchange:
    def __init__(self, grid, send, recv):
        self.grid, self.send, self.recv = grid, send, recv
        self.items, self.unless = [], []

    def copy(self, index):
        offset, src, dst = self.items[index]
        target, ok = peer(self.grid, offset)
        return ok, pltpu.make_async_remote_copy(
            src_ref=src, dst_ref=dst, send_sem=self.send.at[index], recv_sem=self.recv.at[index],
            device_id=target, device_id_type=MESH,
        )

    def add(self, offset, src, dst, unless=None):
        self.items.append((offset, src, dst))
        self.unless.append(unless)
        return len(self.items) - 1

    def sends(self, index):
        ok, copy = self.copy(index)
        unless = self.unless[index]
        return (ok if unless is None else ok & jnp.logical_not(unless)), copy

    def begin(self, index, when=None):
        ok, copy = self.sends(index)
        pl.when(ok if when is None else ok & when)(copy.start)

    def start(self, offset, src, dst, unless=None):
        self.begin(self.add(offset, src, dst, unless))

    def finish_recv(self, index, when=None):
        offset, src, dst = self.items[index]
        _, ok = peer(self.grid, opposite(offset))
        _, copy = self.copy(index)
        pl.when(ok if when is None else ok & when)(copy.wait_recv)
        missing = jnp.logical_not(ok)

        @pl.when(missing if when is None else missing & when)
        def _():
            dst[...] = jnp.zeros(dst.shape, jnp.float32)

    def finish_send(self, index):
        ok, copy = self.sends(index)
        pl.when(ok)(copy.wait_send)


def roll(value, by, axis):
    by = by % value.shape[axis]
    return value if by == 0 else pltpu.roll(value, by, axis)


def iota(shape, dim):
    return lax.broadcasted_iota(jnp.int32, shape, dim)


def row_sums(vol, ysum, first, count):
    row = iota((2, 8, 384), 1)

    def rows(p, _):
        at = pl.ds(first + 2 * p, 2)
        low, high = vol[at, 0:8, :], vol[at, 8:16, :]
        for b in (1, 2, 3):
            up = roll(jnp.where(row < b, high, low), -b, 1)
            down = roll(jnp.where(row >= 8 - b, high, low), b, 1)
            ysum[b - 1, at] = up + down
        return 0

    lax.fori_loop(0, count // 2, rows, 0, unroll=True)


def cone_pair(vol, ysum, x):
    lane = iota((2, 8, 128), 2)
    sums = {}

    def get(b, k):
        return vol[pl.ds(x + k, 2), 0:8, :] if b == 0 else ysum[b - 1, pl.ds(x + k, 2)]

    for a in range(4):
        for b in range(4):
            if a * a + b * b < 12.25:
                sums[a, b] = get(b, 3) if a == 0 else get(b, 3 - a) + get(b, 3 + a)
    groups = {}
    for (a, b), value in sums.items():
        key = (min(a, b), max(a, b))
        groups[key] = groups[key] + value if key in groups else value
    for c in range(4):
        g = None
        for (a, b), value in groups.items():
            w = cone_weight(a, b, c)
            if w > 0:
                g = value * w if g is None else g + value * w
        g0, g1, gh = g[:, :, 0:128], g[:, :, 128:256], g[:, :, 256:384]
        if c == 0:
            t0, t1 = g0, g1
        else:
            t0 = t0 + roll(jnp.where(lane < c, g1, g0), -c, 2) + roll(
                jnp.where(lane >= 128 - c, gh, g0), c, 2)
            t1 = t1 + roll(jnp.where(lane < c, gh, g1), -c, 2) + roll(
                jnp.where(lane >= 128 - c, g0, g1), c, 2)
    return t0, t1


def inverse_weight(grid, out):
    gx, gy, gz = [lax.axis_index(a) for a in AXES]
    y = gy * NY + iota((NY, NZ), 0)
    z = gz * NZ + iota((NY, NZ), 1)

    def pairs(pos, by, size):
        def inside(v):
            return ((v >= 0) & (v < size)).astype(jnp.float32)
        return inside(pos + by) + inside(pos - by) if by else inside(pos)

    ys = [None] + [pairs(y, b, grid[1] * NY) for b in (1, 2, 3)]
    zs = [None] + [pairs(z, c, grid[2] * NZ) for c in (1, 2, 3)]
    fs = []
    for a in range(4):
        f = jnp.full((NY, NZ), 0.0, jnp.float32)
        for b in range(4):
            for c in range(4):
                w = cone_weight(a, b, c)
                if w > 0:
                    term = jnp.float32(w)
                    term = term if b == 0 else term * ys[b]
                    term = term if c == 0 else term * zs[c]
                    f = f + term
        fs.append(f)
    for k in range(14):
        px = gx * NX + k - 3
        w = fs[0] * pairs(px, 0, grid[0] * NX)
        for a in (1, 2, 3):
            w = w + fs[a] * pairs(px, a, grid[0] * NX)
        out[k] = 1.0 / w


def pack_rows(vol, first, half, rows):
    row = iota((8, 256), 0)
    for k in range(half):
        a, b = vol[first + k, 0:8, 0:256], vol[first + half + k, 0:8, 0:256]
        b = roll(b, 4, 0)
        rows[0, k] = jnp.where(row < 4, a, b)
        rows[1, k] = jnp.where(row < 4, b, a)


def pack_thin(vol, rows, node_rows, nodes):
    for p in range(8):
        for f in range(6):
            node_rows[p, f:f + 1, :] = nodes[f, 1 + p, 0:1, :]
        node_rows[p, 6:8, :] = vol[6 + p, 0:2, 0:256]
        for j, r in enumerate((2, 5, 6, 7)):
            rows[j, p:p + 1, :] = vol[6 + p, r:r + 1, 0:256]


def unpack_thin(vol, rows_in, halo):
    row = iota((8, 256), 0)
    for p in range(8):
        value = roll(halo[1 + p, :, 0:256], 2, 0)
        for j, r in enumerate((2, 5, 6, 7)):
            value = jnp.where(row == r, jnp.broadcast_to(rows_in[j, p:p + 1, :], (8, 256)), value)
        vol[6 + p, 8:16, 0:256] = value


def pack_strips(vol, places, slot, pack, nodes):
    lane = iota((8, 128), 1)
    down, up = pack[0], pack[1]
    for i, p in places:
        first, last = vol[p, 0:8, 0:128], vol[p, 0:8, 128:256]
        d, u = roll(first, slot * i, 1), roll(last, slot * i, 1)
        if i == 0:
            down, up = d, u
        else:
            down = jnp.where((lane >= slot * i) & (lane < slot * i + 3), d, down)
            up = jnp.where((lane >= slot * i - 3) & (lane < slot * i), u, up)
        if nodes is not None:
            for f in range(6):
                n = roll(nodes[f, 1 + i, :, 0:128], slot * i + 3 + f, 1)
                down = jnp.where(lane == slot * i + 3 + f, n, down)
    pack[0] = down
    pack[1] = up


def send_strips(ex, pack, strip):
    for o in NEAR:
        _, dy, dz = o
        if dz:
            k = 0 if dz < 0 else 1
            ex.start(o, pack.at[k], strip.at[k, 1 - dy])


def send_rows(ex, rows, rows_in):
    for k, dy in enumerate((-1, 1)):
        ex.start((0, dy, 0), rows.at[k], rows_in.at[k])


def unpack_rows(vol, first, half, rows_in):
    row = iota((8, 256), 0)
    for k in range(half):
        from_upper, from_lower = rows_in[0, k], rows_in[1, k]
        vol[first + k, 8:16, 0:256] = jnp.where(row < 4, from_upper, from_lower)
        vol[first + half + k, 8:16, 0:256] = roll(jnp.where(row < 4, from_lower, from_upper), 4, 0)


def unpack_strips(vol, places, slot, strip):
    rowl = iota((8, 128), 0)
    lane = iota((8, 128), 1)
    both = [jnp.where((lane & (slot - 1)) < slot - 4, strip[0, dy], strip[1, dy]) for dy in range(3)]
    side = jnp.where(rowl < 4, both[2], both[0])
    for i, p in places:
        vol[p, 0:8, 256:384] = roll(both[1], -slot * i, 1)
        vol[p, 8:16, 256:384] = roll(side, -slot * i, 1)
    return both[1], both[2]


def node_halo(halo, main, side):
    lane = iota((8, 128), 1)
    for p in range(8):
        a = roll(main, -(16 * p + 3), 1)
        b = roll(roll(side, -(16 * p + 3) + 8, 1), -1, 0)
        halo[1 + p, :, 256:384] = jnp.where(lane < 8, a, b)


def node_ahead(nodes, ahead, q):
    lane = iota((8, 128), 1)
    for f in range(6):
        v0, v1 = roll(nodes[f, q, :, 0:128], -1, 1), roll(nodes[f, q, :, 128:256], -1, 1)
        ahead[q, f, :, 0:128] = jnp.where(lane == 127, v1, v0)
        ahead[q, f, :, 128:256] = v1


def node_modes(nodes, ahead, halo, halo_up, modes, q):
    lane = iota((8, 128), 1)
    row = iota((8, 128), 0)
    hs = halo[q, :, 256:384]
    hm = jnp.where(row == 7, roll(hs, -8, 1), roll(hs, -1, 0))
    v0, v1 = roll(halo[q, :, 0:128], -1, 1), roll(halo[q, :, 128:256], -1, 1)
    halo_up[q, :, 0:128] = jnp.where(lane == 127, v1, v0)
    halo_up[q, :, 128:256] = v1

    def spread(ref, f, k):
        return jnp.broadcast_to(ref[q, f:f + 1, 128 * k:128 * k + 128], (8, 128))

    for f in range(6):
        for k in range(2):
            at = pl.ds(128 * k, 128)
            n, s = nodes[f, q, :, at], ahead[q, f, :, at]
            e, r = spread(halo, f, k), spread(halo_up, f, k)
            if k == 1:
                s = jnp.where(lane == 127, roll(hs, 127 - f, 1), s)
                r = jnp.where(lane == 127, roll(hm, 127 - f, 1), r)
            a, d = n + s, s - n
            ay = jnp.where(row == 7, e + r, roll(a, -1, 0))
            dy = jnp.where(row == 7, r - e, roll(d, -1, 0))
            modes[q, f, 0, :, at] = a + ay
            modes[q, f, 1, :, at] = d + dy
            modes[q, f, 2, :, at] = ay - a
            modes[q, f, 3, :, at] = dy - d


def element_energy(modes, x, press, mult):
    shear = 1.0 / (2.0 * (1.0 + poisson))
    bulk = 1.0 / (3.0 * (1.0 - 2.0 * poisson))

    def both_of(f, m):
        return modes[x, f, m], modes[x + 1, f, m]

    def field(base):
        out = []
        for c in range(3):
            aa, ad, da, dd = (both_of(base + c, m) for m in range(4))
            out.append(dict(
                X=aa[1] - aa[0], Y=da[0] + da[1], Z=ad[0] + ad[1],
                XY=da[1] - da[0], XZ=ad[1] - ad[0], YZ=dd[0] + dd[1], XYZ=dd[1] - dd[0]))
        return out

    u, l = field(0), field(3)

    def strains(v):
        a, b, c = v
        one = (a["X"], b["Y"], c["Z"], a["Y"] + b["X"], b["Z"] + c["Y"], a["Z"] + c["X"])
        xi = (None, b["XY"], c["XZ"], a["XY"], b["XZ"] + c["XY"], a["XZ"])
        eta = (a["XY"], None, c["YZ"], b["XY"], b["YZ"], a["YZ"] + c["XY"])
        zeta = (a["XZ"], b["YZ"], None, a["YZ"] + b["XZ"], c["YZ"], c["XZ"])
        return one, xi, eta, zeta

    su, sl = strains(u), strains(l)
    total = None
    for kind in range(4):
        eu, el = su[kind], sl[kind]
        normal, tr_u, tr_l = None, None, None
        for k in range(3):
            if eu[k] is not None:
                t = eu[k] * el[k]
                normal = t if normal is None else normal + t
                tr_u = eu[k] if tr_u is None else tr_u + eu[k]
                tr_l = el[k] if tr_l is None else tr_l + el[k]
        gamma = eu[3] * el[3] + eu[4] * el[4] + eu[5] * el[5]
        scale = shear / 16.0 if kind == 0 else shear / 48.0
        part = (2.0 * (normal - tr_u * tr_l * (1.0 / 3.0)) + gamma) * scale
        if kind == 0:
            div_u, div_l = tr_u * 0.25, tr_l * 0.25
        total = part if total is None else total + part
    pure = u[0]["XYZ"] * l[0]["XYZ"] + u[1]["XYZ"] * l[1]["XYZ"] + u[2]["XYZ"] * l[2]["XYZ"]
    total = total + pure * (shear * (10.0 / 3.0) / 144.0)
    return total + div_l * press + mult * div_u - mult * press * (1.0 / bulk)


def kernel(grid, design, flags, disp, adj, press, mult, out,
           vol, vol2, ysum, ysum2, psum, sums_in, rows, rows_in, strip, pack, rows2, rows_in2, rows3, rows_in3, strip2, pack2,
           nodes, node_rows, ahead, halo, halo_up, modes, aux, fl, inv, energy,
           relay, load_sem, ready, leave, pause, onward, send1, recv1, send2, recv2, send3, recv3):
    barrier = pltpu.get_barrier_semaphore()
    at = [lax.axis_index(a) for a in AXES]
    first, last_x, half = 0, grid[0] - 1, grid[0] // 2
    beside = (at[0] == half - 1) | (at[0] == half)
    count = jnp.int32(0)

    def greet(target, ok, counts):
        @pl.when(ok)
        def _():
            pl.semaphore_signal(barrier, inc=1, device_id=target, device_id_type=MESH)

        return count + jnp.int32(1) * counts

    for end in (first, last_x):
        count = greet((end, at[1], at[2]), beside, 2 * (at[0] == end))
    for end, to in ((first, half - 1), (last_x, half)):
        count = greet((to, at[1], at[2]), at[0] == end, at[0] == to)
    own = pl.ds(1, 8)
    loads = [
        (design, vol.at[pl.ds(6, 8), pl.ds(0, 8), pl.ds(0, 256)]),
        (disp, nodes.at[pl.ds(0, 3), own]),
        (adj, nodes.at[pl.ds(3, 3), own]),
        (flags, fl), (press, aux.at[own, 0]), (mult, aux.at[own, 1]),
    ]
    loads = [pltpu.make_async_copy(s, d, load_sem.at[k]) for k, (s, d) in enumerate(loads)]
    for c in loads:
        c.start()
    for o in NEAR:
        target, ok = peer(grid, o)
        count = greet(target, ok, ok)
    for dx in (-1, 1):
        target, ok = peer(grid, (dx, 0, 0))
        ok = ok & (at[0] != (half if dx < 0 else half - 1))
        count = greet(target, ok, ok)
    for c in loads[:3]:
        c.wait()
    own_places = [(i, 6 + i) for i in range(8)]
    pack_strips(vol, own_places, 16, pack, nodes)
    pack_thin(vol, rows, node_rows, nodes)
    pl.semaphore_wait(barrier, count)
    for end, to in ((first, half - 1), (last_x, half)):
        @pl.when(at[0] == end)
        def _():
            pl.semaphore_signal(ready, inc=1, device_id=(to, at[1], at[2]), device_id_type=MESH)

    near = Exchange(grid, send1, recv1)
    send_strips(near, pack, strip)
    near.start((0, -1, 0), node_rows, halo.at[own, :, pl.ds(0, 256)])
    near.start((0, -1, 0), rows.at[pl.ds(0, 1)], rows_in.at[pl.ds(0, 1)])
    near.start((0, 1, 0), rows.at[pl.ds(1, 3)], rows_in.at[pl.ds(1, 3)])
    inverse_weight(grid, inv)
    for c in loads[3:]:
        c.wait()
    for x in range(8):
        aux[1 + x, 2] = jnp.where(fl[x] >= 2, inv[3 + x] * COEF, 0.0)
    lower, upper = (-1, 0, 0), (1, 0, 0)
    far = Exchange(grid, send2, recv2)
    far.start(lower, nodes.at[:, 1], nodes.at[:, 9], at[0] == half)
    far.start(upper, nodes.at[:, 8], nodes.at[:, 0], at[0] == half - 1)
    far.start(upper, aux.at[8], aux.at[0], at[0] == half - 1)
    held, more = relay.at[pl.ds(0, 6)], relay.at[pl.ds(6, 3)]
    ways = [
        (half - 1, first, half, nodes.at[:, 8], held, nodes.at[:, 0], 1),
        (half - 1, first, half, aux.at[8], more, aux.at[0], 2),
        (half, last_x, half - 1, nodes.at[:, 1], held, nodes.at[:, 9], 0),
    ]

    def way(j, leg):
        start, end, to, src, mid, dst, index = ways[j]
        if leg == 0:
            return at[0] == start, at[0] == end, pltpu.make_async_remote_copy(
                src_ref=src, dst_ref=mid, send_sem=leave.at[j], recv_sem=pause.at[j],
                device_id=(end, at[1], at[2]), device_id_type=MESH)
        return at[0] == end, at[0] == to, pltpu.make_async_remote_copy(
            src_ref=mid, dst_ref=dst, send_sem=onward.at[j], recv_sem=recv2.at[index],
            device_id=(to, at[1], at[2]), device_id_type=MESH)

    for j in range(3):
        here, _, copy = way(j, 0)
        pl.when(here)(copy.start)
    for j in range(3):
        _, there, copy = way(j, 0)
        pl.when(there)(copy.wait_recv)
        here, _, copy = way(j, 1)
        pl.when(here)(copy.start)
    sums_in[6:8] = jnp.zeros((2, 8, 256), jnp.float32)
    for k in (0, 14):
        vol[k:k + 6, 0:8, :] = jnp.zeros((6, 8, 384), jnp.float32)
        for b in range(3):
            ysum[b, k:k + 6] = jnp.zeros((6, 8, 384), jnp.float32)

    def own_ahead(q, _):
        node_ahead(nodes, ahead, q)
        return 0

    lax.fori_loop(1, 9, own_ahead, 0)

    for k in range(9):
        near.finish_recv(k)
    for k in range(9):
        near.finish_send(k)
    down_first = at[0] == half
    unpack_thin(vol, rows_in, halo)
    main, side = unpack_strips(vol, own_places, 16, strip)
    node_halo(halo, main, side)

    @pl.when(beside)
    def _():
        pl.semaphore_wait(ready, 1)

    far.start(lower, halo.at[1], halo.at[9])
    far.start(upper, halo.at[8], halo.at[0])
    row_sums(vol, ysum, 6, 8)

    def own_sums(i, _):
        x = jnp.where(down_first, 2 * i, 12 - 2 * i)
        t0, t1 = cone_pair(vol, ysum, x)
        psum[pl.ds(x, 2), :, 0:128] = t0
        psum[pl.ds(x, 2), :, 128:256] = t1
        return 0

    far.add(lower, psum.at[pl.ds(0, 6)], sums_in.at[pl.ds(8, 6)])
    far.add(upper, psum.at[pl.ds(8, 6)], sums_in.at[pl.ds(0, 6)])
    far.add(lower, energy.at[pl.ds(3, 3)], energy.at[pl.ds(11, 3)])
    far.add(upper, energy.at[pl.ds(8, 2)], energy.at[pl.ds(0, 2)])

    def begin(low, high, one):
        far.begin(low, down_first if one else jnp.logical_not(down_first))
        far.begin(high, jnp.logical_not(down_first) if one else down_first)

    lax.fori_loop(0, 3, own_sums, 0, unroll=True)
    begin(5, 6, True)

    def scaled(x):
        return element_energy(modes, x + 1, aux[x + 1, 0], aux[x + 1, 1]) * aux[x + 1, 2]

    def own_modes(i, _):
        node_modes(nodes, ahead, halo, halo_up, modes, jnp.where(down_first, 1 + i, 8 - i))
        return 0

    def energies(i, _):
        x = jnp.where(down_first, i, 6 - i)
        energy[x + 3] = scaled(x)
        return 0

    lax.fori_loop(0, 4, own_modes, 0, unroll=True)
    lax.fori_loop(0, 3, energies, 0, unroll=True)
    begin(7, 8, True)
    lax.fori_loop(3, 7, own_sums, 0)
    begin(5, 6, False)
    lax.fori_loop(4, 8, own_modes, 0)
    lax.fori_loop(3, 7, energies, 0)
    begin(7, 8, False)
    denom = math.tanh(sharpness * threshold) + math.tanh(sharpness * (1.0 - threshold))
    base = math.tanh(sharpness * threshold)
    up_first = jnp.logical_not(down_first)
    last = Exchange(grid, send3, recv3)

    def side_planes(low):
        high = jnp.logical_not(low)
        for k in (1, 2, 4):
            far.finish_recv(k, low)
        for k in (0, 3):
            far.finish_recv(k, high)
        q, x = jnp.where(low, 0, 9), jnp.where(low, -1, 7)
        node_ahead(nodes, ahead, q)
        node_modes(nodes, ahead, halo, halo_up, modes, q)
        energy[x + 3] = scaled(x)
        for k in (6, 8):
            far.finish_recv(k, low)
        for k in (5, 7):
            far.finish_recv(k, high)

    def chain(first, planes):
        for j in range(planes):
            k = first + j
            total = psum[k] + sums_in[k]
            hyper = jnp.tanh(sharpness * (total * inv[k] - threshold))
            smooth = (base + hyper) * (1.0 / denom)
            slope = (1.0 - hyper * hyper) * (sharpness / denom)
            vol2[k, 0:8, 0:256] = smooth * smooth * slope * energy[k]

    early, late = jnp.where(down_first, 6, 0), jnp.where(down_first, 0, 8)
    places = [(i, early + i) for i in range(8)] + [(8 + i, late + i) for i in range(6)]
    side_planes(up_first)
    chain(early, 8)
    pack_rows(vol2, early, 4, rows2)
    send_rows(last, rows2, rows_in2)
    pack_strips(vol2, places[:8], 8, pack2, None)
    side_planes(down_first)
    chain(late, 6)
    pack_strips(vol2, places[8:], 8, pack2, None)
    send_strips(last, pack2, strip2)
    pack_rows(vol2, late, 3, rows3)
    send_rows(last, rows3, rows_in3)
    for ex in (far, last):
        for k in range(len(ex.items)):
            ex.finish_send(k)
    for j in range(3):
        for leg in range(2):
            here, _, copy = way(j, leg)
            pl.when(here)(copy.wait_send)
    for k in (0, 1):
        last.finish_recv(k)
    unpack_rows(vol2, early, 4, rows_in2)
    for k in range(2, 10):
        last.finish_recv(k)
    unpack_strips(vol2, places, 8, strip2)
    unpack_rows(vol2, late, 3, rows_in3)
    row_sums(vol2, ysum2, 0, 14)

    def final(i, _):
        planes = pl.ds(2 * i, 2)
        t0, t1 = cone_pair(vol2, ysum2, 2 * i)
        out[planes, :, 0:128] = jnp.where(fl[planes, :, 0:128] >= 2, t0, 0.0)
        out[planes, :, 128:256] = jnp.where(fl[planes, :, 128:256] >= 2, t1, 0.0)
        return 0

    lax.fori_loop(0, 4, final, 0, unroll=True)


def on_device(grid, *args):
    f32, i32 = jnp.float32, jnp.int32
    V = pltpu.VMEM
    dma = pltpu.SemaphoreType.DMA
    strip, pack = V((2, 3, 8, 128), f32), V((2, 8, 128), f32)
    return pl.pallas_call(
        functools.partial(kernel, grid),
        out_shape=pltpu.VMEM((8, 8, 256), f32),
        in_specs=[pl.BlockSpec(memory_space=pl.ANY)] * 6,
        out_specs=pl.BlockSpec(memory_space=pltpu.VMEM),
        scratch_shapes=[
            V((20, 16, 384), f32), V((14, 16, 384), f32), V((3, 20, 8, 384), f32), V((3, 14, 8, 384), f32),
            V((14, 8, 256), f32), V((14, 8, 256), f32),
            V((4, 8, 256), f32), V((4, 8, 256), f32), strip, pack,
            V((2, 4, 8, 256), f32), V((2, 4, 8, 256), f32), V((2, 3, 8, 256), f32), V((2, 3, 8, 256), f32), strip, pack,
            V((6, 10, 8, 256), f32), V((8, 8, 256), f32), V((10, 6, 8, 256), f32), V((10, 8, 384), f32), V((10, 8, 256), f32),
            V((10, 6, 4, 8, 256), f32),
            V((9, 3, 8, 256), f32), V((8, 8, 256), i32), V((14, 8, 256), f32), V((14, 8, 256), f32),
            V((9, 8, 256), f32),
            dma((6,)), pltpu.SemaphoreType.REGULAR, dma((3,)), dma((3,)), dma((3,)), dma((9,)), dma((9,)), dma((9,)), dma((9,)), dma((10,)), dma((10,)),
        ],
        compiler_params=pltpu.CompilerParams(
            collective_id=0, has_side_effects=True, vmem_limit_bytes=63 << 20),
        name="sensitivity",
    )(*args)


def solution(mesh):
    grid = tuple(mesh.shape[a] for a in AXES)
    brick = P("gx", "gy", "gz")
    field = P(None, "gx", "gy", "gz")
    return jax.shard_map(
        functools.partial(on_device, grid), mesh=mesh,
        in_specs=(brick, brick, field, field, brick, brick), out_specs=brick, check_vma=False,
    )
```

time: 25.5 us -> 25 us (0.980)
  Pallas kernels: 24.8 us -> 24.2 us
    pallas_call x1, Pallas kernels: 24.8 us -> 24.2 us  [on_device(): pl.pallas_call(functools.partial(kernel, grid), out_shape=pltpu.VMEM((8,...]
where the time goes in v5:
time: 25 us; the launch traced here: 24.9 us
  Pallas kernels  24.2 us (97%)
  local copies, waits for them, and re-layouts  0.63 us (3%)
    pallas_call x1, Pallas kernels, on_device(): pl.pallas_call(functools.partial(kernel, grid), out_shape=pltpu.VMEM((8,...  24.2 us
    unnamed x1, local copies, waits for them, and re-layouts  0.63 us

profile of v5, /device:TPU:199, one launch (start us, length us, event | category | flops | bytes accessed | tf_op | source)
XLA Modules:
  0.0 24.9 jit_solution(14968959960049613869)
XLA Ops:
  0.0 24.2 %sensitivity.1 = f32[8,8,256]{2,1,0:T(8,128)S(1)} custom-call(f32[8,8,256]{2,1,0:T(8,128)} %design.1, s32[8,8,256]{2,1,0:T(8,128)} %flags.1, f32[3,8,8,256]{3,2,1,0:T(8,128)} %disp.1, f32[3,8,8,256]{3,2,1,0:T(8,128)} %adj.1, f32[8,8,256]{2,1,0:T(8,128)} %press.1, f32[8,8,256]{2,1,0:T(8,128)} %mult.1), custom_call_target="tpu_custom_call" | custom-call | tf_op jit(solution)/shard_map/sensitivity/pallas_call | solution.py:584
  24.2 0.6 %copy.8 = f32[8,8,256]{2,1,0:T(8,128)} copy(f32[8,8,256]{2,1,0:T(8,128)S(1)} %sensitivity.1) | data formatting | bytes 131072

commit v6 on v5

--- a/solution.py
+++ b/solution.py
@@ -87,9 +87,9 @@
         def _():
             dst[...] = jnp.zeros(dst.shape, jnp.float32)
 
-    def finish_send(self, index):
+    def finish_send(self, index, done=None):
         ok, copy = self.sends(index)
-        pl.when(ok)(copy.wait_send)
+        pl.when(ok if done is None else ok & jnp.logical_not(done))(copy.wait_send)
 
 
 def roll(value, by, axis):
@@ -101,27 +101,28 @@
     return lax.broadcasted_iota(jnp.int32, shape, dim)
 
 
-def row_sums(vol, ysum, first, count):
-    row = iota((2, 8, 384), 1)
+def row_sums(vol, ysum, first, count, lanes=(0, 384)):
+    at, wide = pl.ds(lanes[0], lanes[1] - lanes[0]), lanes[1] - lanes[0]
+    row = iota((2, 8, wide), 1)
 
     def rows(p, _):
-        at = pl.ds(first + 2 * p, 2)
-        low, high = vol[at, 0:8, :], vol[at, 8:16, :]
+        planes = pl.ds(first + 2 * p, 2)
+        low, high = vol[planes, 0:8, at], vol[planes, 8:16, at]
         for b in (1, 2, 3):
             up = roll(jnp.where(row < b, high, low), -b, 1)
             down = roll(jnp.where(row >= 8 - b, high, low), b, 1)
-            ysum[b - 1, at] = up + down
+            ysum[b - 1, planes, :, at] = up + down
         return 0
 
     lax.fori_loop(0, count // 2, rows, 0, unroll=True)
 
 
-def cone_pair(vol, ysum, x):
-    lane = iota((2, 8, 128), 2)
+def plane_sums(vol, ysum, x, lanes):
+    at = pl.ds(lanes[0], lanes[1] - lanes[0])
     sums = {}
 
     def get(b, k):
-        return vol[pl.ds(x + k, 2), 0:8, :] if b == 0 else ysum[b - 1, pl.ds(x + k, 2)]
+        return vol[pl.ds(x + k, 2), 0:8, at] if b == 0 else ysum[b - 1, pl.ds(x + k, 2), :, at]
 
     for a in range(4):
         for b in range(4):
@@ -131,12 +132,20 @@
     for (a, b), value in sums.items():
         key = (min(a, b), max(a, b))
         groups[key] = groups[key] + value if key in groups else value
+    shifted = []
     for c in range(4):
         g = None
         for (a, b), value in groups.items():
             w = cone_weight(a, b, c)
             if w > 0:
                 g = value * w if g is None else g + value * w
+        shifted.append(g)
+    return shifted
+
+
+def cone_pair(vol, ysum, x):
+    lane = iota((2, 8, 128), 2)
+    for c, g in enumerate(plane_sums(vol, ysum, x, (0, 384))):
         g0, g1, gh = g[:, :, 0:128], g[:, :, 128:256], g[:, :, 256:384]
         if c == 0:
             t0, t1 = g0, g1
@@ -145,6 +154,30 @@
                 jnp.where(lane >= 128 - c, gh, g0), c, 2)
             t1 = t1 + roll(jnp.where(lane < c, gh, g1), -c, 2) + roll(
                 jnp.where(lane >= 128 - c, g0, g1), c, 2)
+    return t0, t1
+
+
+def cone_inner(vol, ysum, x):
+    lane = iota((2, 8, 128), 2)
+    for c, g in enumerate(plane_sums(vol, ysum, x, (0, 256))):
+        g0, g1 = g[:, :, 0:128], g[:, :, 128:256]
+        if c == 0:
+            t0, t1 = g0, g1
+        else:
+            t0 = t0 + roll(jnp.where(lane < c, g1, g0), -c, 2) + roll(
+                jnp.where(lane >= 128 - c, 0.0, g0), c, 2)
+            t1 = t1 + roll(jnp.where(lane < c, 0.0, g1), -c, 2) + roll(
+                jnp.where(lane >= 128 - c, g0, g1), c, 2)
+    return t0, t1
+
+
+def cone_halo(vol, ysum, x):
+    lane = iota((2, 8, 128), 2)
+    t0, t1 = 0.0, 0.0
+    for c, g in enumerate(plane_sums(vol, ysum, x, (256, 384))):
+        if c:
+            t0 = t0 + roll(jnp.where(lane >= 128 - c, g, 0.0), c, 2)
+            t1 = t1 + roll(jnp.where(lane < c, g, 0.0), -c, 2)
     return t0, t1
 
 
@@ -193,17 +226,18 @@
     for p in range(8):
         for f in range(6):
             node_rows[p, f:f + 1, :] = nodes[f, 1 + p, 0:1, :]
-        node_rows[p, 6:8, :] = vol[6 + p, 0:2, 0:256]
-        for j, r in enumerate((2, 5, 6, 7)):
+        node_rows[p, 6:8, :] = jnp.zeros((2, 256), jnp.float32)
+        for j, r in enumerate((0, 1, 2, 5, 6, 7)):
             rows[j, p:p + 1, :] = vol[6 + p, r:r + 1, 0:256]
 
 
-def unpack_thin(vol, rows_in, halo):
+def unpack_thin(vol, rows_in):
     row = iota((8, 256), 0)
     for p in range(8):
-        value = roll(halo[1 + p, :, 0:256], 2, 0)
-        for j, r in enumerate((2, 5, 6, 7)):
-            value = jnp.where(row == r, jnp.broadcast_to(rows_in[j, p:p + 1, :], (8, 256)), value)
+        value = None
+        for j, r in enumerate((0, 1, 2, 5, 6, 7)):
+            here = jnp.broadcast_to(rows_in[j, p:p + 1, :], (8, 256))
+            value = here if value is None else jnp.where(row == r, here, value)
         vol[6 + p, 8:16, 0:256] = value
 
 
@@ -352,9 +386,9 @@
 
 
 def kernel(grid, design, flags, disp, adj, press, mult, out,
-           vol, vol2, ysum, ysum2, psum, sums_in, rows, rows_in, strip, pack, rows2, rows_in2, rows3, rows_in3, strip2, pack2,
+           vol, vol2, ysum, ysum2, inner, psum, sums_in, rows, rows_in, strip, pack, rows2, rows_in2, rows3, rows_in3, strip2, pack2,
            nodes, node_rows, ahead, halo, halo_up, modes, aux, fl, inv, energy,
-           relay, load_sem, ready, leave, pause, onward, send1, recv1, send2, recv2, send3, recv3):
+           relay, blank, edge_out, edge_in, load_sem, ready, leave, pause, onward, send1, recv1, send2, recv2, send3, recv3):
     barrier = pltpu.get_barrier_semaphore()
     at = [lax.axis_index(a) for a in AXES]
     first, last_x, half = 0, grid[0] - 1, grid[0] // 2
@@ -380,7 +414,7 @@
         (flags, fl), (press, aux.at[own, 0]), (mult, aux.at[own, 1]),
     ]
     loads = [pltpu.make_async_copy(s, d, load_sem.at[k]) for k, (s, d) in enumerate(loads)]
-    for c in loads:
+    for c in loads[:3]:
         c.start()
     for o in NEAR:
         target, ok = peer(grid, o)
@@ -391,6 +425,8 @@
         count = greet(target, ok, ok)
     for c in loads[:3]:
         c.wait()
+    for c in loads[3:]:
+        c.start()
     own_places = [(i, 6 + i) for i in range(8)]
     pack_strips(vol, own_places, 16, pack, nodes)
     pack_thin(vol, rows, node_rows, nodes)
@@ -402,9 +438,9 @@
 
     near = Exchange(grid, send1, recv1)
     send_strips(near, pack, strip)
+    near.start((0, -1, 0), rows.at[pl.ds(0, 3)], rows_in.at[pl.ds(0, 3)])
+    near.start((0, 1, 0), rows.at[pl.ds(3, 3)], rows_in.at[pl.ds(3, 3)])
     near.start((0, -1, 0), node_rows, halo.at[own, :, pl.ds(0, 256)])
-    near.start((0, -1, 0), rows.at[pl.ds(0, 1)], rows_in.at[pl.ds(0, 1)])
-    near.start((0, 1, 0), rows.at[pl.ds(1, 3)], rows_in.at[pl.ds(1, 3)])
     inverse_weight(grid, inv)
     for c in loads[3:]:
         c.wait()
@@ -452,21 +488,48 @@
 
     lax.fori_loop(1, 9, own_ahead, 0)
 
-    for k in range(9):
+    down_first = at[0] == half
+    def scaled(x):
+        return element_energy(modes, x + 1, aux[x + 1, 0], aux[x + 1, 1]) * aux[x + 1, 2]
+
+    def own_modes(i, _):
+        node_modes(nodes, ahead, halo, halo_up, modes, jnp.where(down_first, 1 + i, 8 - i))
+        return 0
+
+    def first_modes(i, _):
+        node_modes(nodes, ahead, blank, halo_up, modes, jnp.where(down_first, 1 + i, 8 - i))
+        return 0
+
+    def energies(i, _):
+        x = jnp.where(down_first, i, 6 - i)
+        energy[x + 3] = scaled(x)
+        return 0
+
+
+    @pl.when(beside)
+    def _():
+        blank[...] = jnp.zeros(blank.shape, jnp.float32)
+        lax.fori_loop(0, 4, first_modes, 0, unroll=True)
+        lax.fori_loop(0, 3, energies, 0, unroll=True)
+        pl.semaphore_wait(ready, 1)
+
+    for k in (3, 4):
+        far.add(*((lower, halo.at[1], halo.at[9]) if k == 3 else (upper, halo.at[8], halo.at[0])))
+    far.add(lower, psum.at[pl.ds(0, 6)], sums_in.at[pl.ds(8, 6)])
+    far.add(upper, psum.at[pl.ds(8, 6)], sums_in.at[pl.ds(0, 6)])
+    far.add(lower, energy.at[pl.ds(3, 3)], energy.at[pl.ds(11, 3)])
+    far.add(upper, energy.at[pl.ds(8, 2)], energy.at[pl.ds(0, 2)])
+    far.add(lower, edge_out, edge_in, at[0] != half)
+    far.add(upper, edge_out, edge_in, at[0] != half - 1)
+    far.begin(7, at[0] == half)
+    far.begin(8, at[0] == half - 1)
+
+    for k in range(8):
         near.finish_recv(k)
-    for k in range(9):
-        near.finish_send(k)
-    down_first = at[0] == half
-    unpack_thin(vol, rows_in, halo)
+    unpack_thin(vol, rows_in)
     main, side = unpack_strips(vol, own_places, 16, strip)
     node_halo(halo, main, side)
 
-    @pl.when(beside)
-    def _():
-        pl.semaphore_wait(ready, 1)
-
-    far.start(lower, halo.at[1], halo.at[9])
-    far.start(upper, halo.at[8], halo.at[0])
     row_sums(vol, ysum, 6, 8)
 
     def own_sums(i, _):
@@ -476,10 +539,6 @@
         psum[pl.ds(x, 2), :, 128:256] = t1
         return 0
 
-    far.add(lower, psum.at[pl.ds(0, 6)], sums_in.at[pl.ds(8, 6)])
-    far.add(upper, psum.at[pl.ds(8, 6)], sums_in.at[pl.ds(0, 6)])
-    far.add(lower, energy.at[pl.ds(3, 3)], energy.at[pl.ds(11, 3)])
-    far.add(upper, energy.at[pl.ds(8, 2)], energy.at[pl.ds(0, 2)])
 
     def begin(low, high, one):
         far.begin(low, down_first if one else jnp.logical_not(down_first))
@@ -487,22 +546,32 @@
 
     lax.fori_loop(0, 3, own_sums, 0, unroll=True)
     begin(5, 6, True)
-
-    def scaled(x):
-        return element_energy(modes, x + 1, aux[x + 1, 0], aux[x + 1, 1]) * aux[x + 1, 2]
-
-    def own_modes(i, _):
-        node_modes(nodes, ahead, halo, halo_up, modes, jnp.where(down_first, 1 + i, 8 - i))
-        return 0
-
-    def energies(i, _):
-        x = jnp.where(down_first, i, 6 - i)
-        energy[x + 3] = scaled(x)
-        return 0
+    near.finish_recv(8)
+    for k in (3, 4):
+        far.begin(k)
+    for k in range(9):
+        near.finish_send(k)
 
     lax.fori_loop(0, 4, own_modes, 0, unroll=True)
+    for ex, low in ((7, True), (8, False)):
+        pl.when(beside & (down_first if low else jnp.logical_not(down_first)))(far.sends(ex)[1].wait_send)
     lax.fori_loop(0, 3, energies, 0, unroll=True)
-    begin(7, 8, True)
+
+    @pl.when(beside)
+    def _():
+        lane = iota((8, 128), 1)
+        first_plane = jnp.where(down_first, 3, 8)
+        strip_of = None
+        for j in range(3):
+            edge_out[j:j + 1, 0:256] = energy[first_plane + j, 7:8, :]
+            moved = roll(energy[first_plane + j, :, 128:256], j - 127, 1)
+            strip_of = moved if j == 0 else jnp.where(lane == j, moved, strip_of)
+        edge_out[:, 256:384] = strip_of
+
+    far.begin(9)
+    far.begin(10)
+    far.begin(7, jnp.logical_not(beside) & down_first)
+    far.begin(8, jnp.logical_not(beside) & jnp.logical_not(down_first))
     lax.fori_loop(3, 7, own_sums, 0)
     begin(5, 6, False)
     lax.fori_loop(4, 8, own_modes, 0)
@@ -528,6 +597,18 @@
         for k in (5, 7):
             far.finish_recv(k, high)
 
+    def put_edge():
+        far.finish_recv(9, at[0] == half - 1)
+        far.finish_recv(10, at[0] == half)
+        row, lane = iota((8, 256), 0), iota((8, 256), 1)
+        for j in range(3):
+            @pl.when(beside & up_first if j == 2 else beside)
+            def _():
+                k = jnp.where(down_first, 0, 11) + j
+                edge = roll(edge_in[:, 256:384], 127 - j, 1)
+                value = jnp.where(lane == 255, jnp.concatenate([edge, edge], axis=1), energy[k])
+                energy[k] = jnp.where(row == 7, jnp.broadcast_to(edge_in[j:j + 1, 0:256], (8, 256)), value)
+
     def chain(first, planes):
         for j in range(planes):
             k = first + j
@@ -545,6 +626,7 @@
     send_rows(last, rows2, rows_in2)
     pack_strips(vol2, places[:8], 8, pack2, None)
     side_planes(down_first)
+    put_edge()
     chain(late, 6)
     pack_strips(vol2, places[8:], 8, pack2, None)
     send_strips(last, pack2, strip2)
@@ -552,7 +634,8 @@
     send_rows(last, rows3, rows_in3)
     for ex in (far, last):
         for k in range(len(ex.items)):
-            ex.finish_send(k)
+            done = beside & (down_first if k == 7 else up_first) if ex is far and k in (7, 8) else None
+            ex.finish_send(k, done)
     for j in range(3):
         for leg in range(2):
             here, _, copy = way(j, leg)
@@ -560,20 +643,24 @@
     for k in (0, 1):
         last.finish_recv(k)
     unpack_rows(vol2, early, 4, rows_in2)
-    for k in range(2, 10):
+    for k in (8, 9):
+        last.finish_recv(k)
+    unpack_rows(vol2, late, 3, rows_in3)
+    row_sums(vol2, ysum2, 0, 14, (0, 256))
+    for i in range(4):
+        planes = pl.ds(2 * i, 2)
+        t0, t1 = cone_inner(vol2, ysum2, 2 * i)
+        inner[planes, :, 0:128] = t0
+        inner[planes, :, 128:256] = t1
+    for k in range(2, 8):
         last.finish_recv(k)
     unpack_strips(vol2, places, 8, strip2)
-    unpack_rows(vol2, late, 3, rows_in3)
-    row_sums(vol2, ysum2, 0, 14)
-
-    def final(i, _):
+    row_sums(vol2, ysum2, 0, 14, (256, 384))
+    for i in range(4):
         planes = pl.ds(2 * i, 2)
-        t0, t1 = cone_pair(vol2, ysum2, 2 * i)
-        out[planes, :, 0:128] = jnp.where(fl[planes, :, 0:128] >= 2, t0, 0.0)
-        out[planes, :, 128:256] = jnp.where(fl[planes, :, 128:256] >= 2, t1, 0.0)
-        return 0
-
-    lax.fori_loop(0, 4, final, 0, unroll=True)
+        for half_at, t in zip((0, 128), cone_halo(vol2, ysum2, 2 * i)):
+            lanes = pl.ds(half_at, 128)
+            out[planes, :, lanes] = jnp.where(fl[planes, :, lanes] >= 2, inner[planes, :, lanes] + t, 0.0)
 
 
 def on_device(grid, *args):
@@ -587,15 +674,15 @@
         in_specs=[pl.BlockSpec(memory_space=pl.ANY)] * 6,
         out_specs=pl.BlockSpec(memory_space=pltpu.VMEM),
         scratch_shapes=[
-            V((20, 16, 384), f32), V((14, 16, 384), f32), V((3, 20, 8, 384), f32), V((3, 14, 8, 384), f32),
+            V((20, 16, 384), f32), V((14, 16, 384), f32), V((3, 20, 8, 384), f32), V((3, 14, 8, 384), f32), V((8, 8, 256), f32),
             V((14, 8, 256), f32), V((14, 8, 256), f32),
-            V((4, 8, 256), f32), V((4, 8, 256), f32), strip, pack,
+            V((6, 8, 256), f32), V((6, 8, 256), f32), strip, pack,
             V((2, 4, 8, 256), f32), V((2, 4, 8, 256), f32), V((2, 3, 8, 256), f32), V((2, 3, 8, 256), f32), strip, pack,
             V((6, 10, 8, 256), f32), V((8, 8, 256), f32), V((10, 6, 8, 256), f32), V((10, 8, 384), f32), V((10, 8, 256), f32),
             V((10, 6, 4, 8, 256), f32),
             V((9, 3, 8, 256), f32), V((8, 8, 256), i32), V((14, 8, 256), f32), V((14, 8, 256), f32),
-            V((9, 8, 256), f32),
-            dma((6,)), pltpu.SemaphoreType.REGULAR, dma((3,)), dma((3,)), dma((3,)), dma((9,)), dma((9,)), dma((9,)), dma((9,)), dma((10,)), dma((10,)),
+            V((9, 8, 256), f32), V((10, 8, 384), f32), V((8, 384), f32), V((8, 384), f32),
+            dma((6,)), pltpu.SemaphoreType.REGULAR, dma((3,)), dma((3,)), dma((3,)), dma((9,)), dma((9,)), dma((11,)), dma((11,)), dma((10,)), dma((10,)),
         ],
         compiler_params=pltpu.CompilerParams(
             collective_id=0, has_side_effects=True, vmem_limit_bytes=63 << 20),

time: 25 us -> 24.8 us (level)
  no operation moved by 1% of the time
where the time goes in v6:
time: 24.8 us; the launch traced here: 24.7 us
  Pallas kernels  24 us (97%)
  local copies, waits for them, and re-layouts  0.63 us (3%)
    pallas_call x1, Pallas kernels, on_device(): pl.pallas_call(functools.partial(kernel, grid), out_shape=pltpu.VMEM((8,...  24 us
    unnamed x1, local copies, waits for them, and re-layouts  0.63 us

profile of v6, /device:TPU:199, one launch (start us, length us, event | category | flops | bytes accessed | tf_op | source)
XLA Modules:
  0.0 24.7 jit_solution(1835540607746262253)
XLA Ops:
  0.0 24.0 %sensitivity.1 = f32[8,8,256]{2,1,0:T(8,128)S(1)} custom-call(f32[8,8,256]{2,1,0:T(8,128)} %design.1, s32[8,8,256]{2,1,0:T(8,128)} %flags.1, f32[3,8,8,256]{3,2,1,0:T(8,128)} %disp.1, f32[3,8,8,256]{3,2,1,0:T(8,128)} %adj.1, f32[8,8,256]{2,1,0:T(8,128)} %press.1, f32[8,8,256]{2,1,0:T(8,128)} %mult.1), custom_call_target="tpu_custom_call" | custom-call | tf_op jit(solution)/shard_map/sensitivity/pallas_call | solution.py:671
  24.0 0.6 %copy.8 = f32[8,8,256]{2,1,0:T(8,128)} copy(f32[8,8,256]{2,1,0:T(8,128)S(1)} %sensitivity.1) | data formatting | bytes 131072

commit v7 on v6

--- a/solution.py
+++ b/solution.py
@@ -486,7 +486,7 @@
         node_ahead(nodes, ahead, q)
         return 0
 
-    lax.fori_loop(1, 9, own_ahead, 0)
+    lax.fori_loop(1, 9, own_ahead, 0, unroll=True)
 
     down_first = at[0] == half
     def scaled(x):
@@ -572,10 +572,10 @@
     far.begin(10)
     far.begin(7, jnp.logical_not(beside) & down_first)
     far.begin(8, jnp.logical_not(beside) & jnp.logical_not(down_first))
-    lax.fori_loop(3, 7, own_sums, 0)
+    lax.fori_loop(3, 7, own_sums, 0, unroll=True)
     begin(5, 6, False)
-    lax.fori_loop(4, 8, own_modes, 0)
-    lax.fori_loop(3, 7, energies, 0)
+    lax.fori_loop(4, 8, own_modes, 0, unroll=True)
+    lax.fori_loop(3, 7, energies, 0, unroll=True)
     begin(7, 8, False)
     denom = math.tanh(sharpness * threshold) + math.tanh(sharpness * (1.0 - threshold))
     base = math.tanh(sharpness * threshold)

time: 24.8 us -> 24.7 us (level)
  no operation moved by 1% of the time
where the time goes in v7:
time: 24.7 us; the launch traced here: 24.5 us
  Pallas kernels  23.9 us (97%)
  local copies, waits for them, and re-layouts  0.63 us (3%)
    pallas_call x1, Pallas kernels, on_device(): pl.pallas_call(functools.partial(kernel, grid), out_shape=pltpu.VMEM((8,...  23.9 us
    unnamed x1, local copies, waits for them, and re-layouts  0.63 us

profile of v7, /device:TPU:199, one launch (start us, length us, event | category | flops | bytes accessed | tf_op | source)
XLA Modules:
  0.0 24.5 jit_solution(17689515754772307427)
XLA Ops:
  0.0 23.9 %sensitivity.1 = f32[8,8,256]{2,1,0:T(8,128)S(1)} custom-call(f32[8,8,256]{2,1,0:T(8,128)} %design.1, s32[8,8,256]{2,1,0:T(8,128)} %flags.1, f32[3,8,8,256]{3,2,1,0:T(8,128)} %disp.1, f32[3,8,8,256]{3,2,1,0:T(8,128)} %adj.1, f32[8,8,256]{2,1,0:T(8,128)} %press.1, f32[8,8,256]{2,1,0:T(8,128)} %mult.1), custom_call_target="tpu_custom_call" | custom-call | tf_op jit(solution)/shard_map/sensitivity/pallas_call | solution.py:671
  23.9 0.6 %copy.8 = f32[8,8,256]{2,1,0:T(8,128)} copy(f32[8,8,256]{2,1,0:T(8,128)S(1)} %sensitivity.1) | data formatting | bytes 131072

commit v8 on v7

--- a/solution.py
+++ b/solution.py
@@ -547,10 +547,7 @@
     lax.fori_loop(0, 3, own_sums, 0, unroll=True)
     begin(5, 6, True)
     near.finish_recv(8)
-    for k in (3, 4):
-        far.begin(k)
-    for k in range(9):
-        near.finish_send(k)
+    begin(3, 4, True)
 
     lax.fori_loop(0, 4, own_modes, 0, unroll=True)
     for ex, low in ((7, True), (8, False)):
@@ -570,6 +567,7 @@
 
     far.begin(9)
     far.begin(10)
+    begin(3, 4, False)
     far.begin(7, jnp.logical_not(beside) & down_first)
     far.begin(8, jnp.logical_not(beside) & jnp.logical_not(down_first))
     lax.fori_loop(3, 7, own_sums, 0, unroll=True)
@@ -632,7 +630,7 @@
     send_strips(last, pack2, strip2)
     pack_rows(vol2, late, 3, rows3)
     send_rows(last, rows3, rows_in3)
-    for ex in (far, last):
+    for ex in (near, far, last):
         for k in range(len(ex.items)):
             done = beside & (down_first if k == 7 else up_first) if ex is far and k in (7, 8) else None
             ex.finish_send(k, done)

time: 24.7 us -> 24.7 us (level)
  no operation moved by 1% of the time
where the time goes in v8:
time: 24.7 us; the launch traced here: 24.5 us
  Pallas kernels  23.9 us (97%)
  local copies, waits for them, and re-layouts  0.63 us (3%)
    pallas_call x1, Pallas kernels, on_device(): pl.pallas_call(functools.partial(kernel, grid), out_shape=pltpu.VMEM((8,...  23.9 us
    unnamed x1, local copies, waits for them, and re-layouts  0.63 us

profile of v8, /device:TPU:199, one launch (start us, length us, event | category | flops | bytes accessed | tf_op | source)
XLA Modules:
  0.0 24.5 jit_solution(700597732216365645)
XLA Ops:
  0.0 23.9 %sensitivity.1 = f32[8,8,256]{2,1,0:T(8,128)S(1)} custom-call(f32[8,8,256]{2,1,0:T(8,128)} %design.1, s32[8,8,256]{2,1,0:T(8,128)} %flags.1, f32[3,8,8,256]{3,2,1,0:T(8,128)} %disp.1, f32[3,8,8,256]{3,2,1,0:T(8,128)} %adj.1, f32[8,8,256]{2,1,0:T(8,128)} %press.1, f32[8,8,256]{2,1,0:T(8,128)} %mult.1), custom_call_target="tpu_custom_call" | custom-call | tf_op jit(solution)/shard_map/sensitivity/pallas_call | solution.py:669
  23.9 0.6 %copy.8 = f32[8,8,256]{2,1,0:T(8,128)} copy(f32[8,8,256]{2,1,0:T(8,128)S(1)} %sensitivity.1) | data formatting | bytes 131072
